TPU v7x, 512 devices: a whole 4x8x8 slice. The times are simulated.
512 devices in a mesh: rep: 16 (over x, z_lo), fsdp: 32 (over z_hi, y, core).
Axes of the slice: x: 4, y: 8, z: 8 (z_hi: 2, z_lo: 4; z = z_hi * 4 + z_lo), core: 2. Of those that a mesh axis runs over, the one named last changes fastest.
Arguments:
- activations: bfloat16 [2048, 8192], P('fsdp', 'rep'), may hold values from -6 to 6
- out_grads: bfloat16 [2048, 32768], P('rep', 'fsdp'), may hold values from -0.19921875 to 0.19921875
- in_basis: bfloat16 [8192, 512], P('rep', 'fsdp'), may hold values from -0.25 to 0.25
- out_basis: bfloat16 [32768, 1024], P('fsdp', 'rep'), may hold values from -0.1875 to 0.1875
Outputs:
- scaled_grad: float32 [8192, 32768], P('rep', 'fsdp')
All inputs are finite; a program needn't handle non-finite values.
Results may differ from a plain program's by a relative error of at most 0.0041.
Values may be sent and summed in bfloat16 or wider, within the bound.
A program may use at most 64 MiB of HBM per device.

v0:
```python
import jax
import jax.numpy as jnp
from jax import lax
from jax.sharding import PartitionSpec as P

BA = 512
BG = 1024


damping = 0.001


def rotate(block, blocks):
    count = block.shape[0]
    nblocks, width, _ = blocks.shape
    parts = block.reshape(count, nblocks, width)
    turned = jnp.einsum("tkb,kbc->tkc", parts, blocks, preferred_element_type=jnp.float32)
    return turned.reshape(count, nblocks * width).astype(jnp.bfloat16)


def per_device(activations, out_grads, in_basis, out_basis):
    in_cols = lax.all_gather(in_basis, "fsdp", axis=1, tiled=True)
    in_blocks = in_cols.reshape(-1, BA, BA)
    rot_x = rotate(lax.all_gather(activations, "fsdp", axis=0, tiled=True), in_blocks)
    sq_x = (rot_x.astype(jnp.float32) ** 2).astype(jnp.bfloat16)
    tokens = rot_x.shape[0]
    contract = (((0,), (0,)), ((), ()))
    out_cols = lax.all_gather(out_basis, "rep", axis=1, tiled=True)
    rot_g = rotate(out_grads, out_cols.reshape(-1, BG, BG))
    piece = lax.all_gather(rot_g, "rep", axis=0, tiled=True)
    gs_part = (piece.astype(jnp.float32) ** 2).astype(jnp.bfloat16)
    scale_part = lax.dot_general(sq_x, gs_part, contract, preferred_element_type=jnp.float32)
    grad_part = lax.dot_general(rot_x, piece, contract, preferred_element_type=jnp.float32)
    total = float(tokens)
    return grad_part / total / (scale_part / total + damping)


def solution(mesh):
    in_specs = (P("fsdp", "rep"), P("rep", "fsdp"), P("rep", "fsdp"), P("fsdp", "rep"))
    out_specs = P("rep", "fsdp")
    return jax.shard_map(
        per_device, mesh=mesh, in_specs=in_specs, out_specs=out_specs, check_vma=False
    )
```

profile of v0, /device:TPU:56, one launch (start us, length us, event | category | flops | bytes accessed | tf_op | source)
XLA Modules:
  0.0 324.1 jit_solution(988073812477402194)
XLA Ops:
  6.5 0.0 copy-start
  6.5 0.0 copy-start.1
  6.5 0.0 all-gather.7.cloned.1.call-start
  6.5 0.7 all-gather.7.cloned.1.call-update
  7.3 0.0 all-gather.5.cloned.1.call-start
  7.3 0.7 all-gather.5.cloned.1.call-update
  8.0 0.0 all-gather.9.cloned.1.call-start
  8.1 95.4 %all-gather.7.cloned.1.call-done = bf16[1024,1024]{0,1:T(8,128)(2,1)} async-done(((bf16[1024,64]{0,1:T(8,128)(2,1)}), bf16[1024,1024]{0,1:T(8,128)(2,1)}) %all-gather.7.cloned.1.call-update) | async-done | bytes 2097168 | tf_op jit(solution)/shard_map/all_gather | solution.py:28
  103.4 0.0 copy-done
  103.4 3.0 fusion.7
  106.4 0.0 all-gather.9.cloned.1.call-update
  106.4 0.0 copy-done.1
  106.5 47.3 %all_gather.12 = bf16[512,512]{0,1:T(8,128)(2,1)S(1)} all-gather(bf16[512,16]{0,1:T(8,128)(2,1)S(1)} %copy-done.1), channel_id=1, replica_groups=mesh['rep'=16,'fsdp'=32] {'fsdp'}, dimensions={1}, use_global_device_ids=true | all-gather | bytes 540672 | tf_op jit(solution)/shard_map/all_gather | solution.py:22
  153.8 45.1 %all-gather.5.cloned.1.call-done = bf16[2048,512]{1,0:T(8,128)(2,1)} async-done(((bf16[64,512]{1,0:T(8,128)(2,1)}), bf16[2048,512]{1,0:T(8,128)(2,1)}) %all-gather.5.cloned.1.call-update) | async-done | bytes 2097168 | tf_op jit(solution)/shard_map/all_gather | solution.py:24
  198.9 2.9 fusion.4
  201.8 107.2 %all-gather.9.cloned.1.call-done = bf16[2048,1,1024]{0,2,1:T(8,128)(2,1)} async-done(((bf16[128,1,1024]{0,2,1:T(8,128)(2,1)}), bf16[2048,1,1024]{0,2,1:T(8,128)(2,1)}) %all-gather.9.cloned.1.call-update) | async-done | bytes 4194320 | tf_op jit(solution)/shard_map/all_gather | solution.py:30
  309.0 0.0 copy-start.2
  309.0 4.7 %fusion = f32[512,1024]{1,0:T(8,128)S(1)} fusion(bf16[2048,1,1024]{0,2,1:T(8,128)(2,1)} %all-gather.9.cloned.1.call-done, bf16[2048,512]{0,1:T(8,128)(2,1)S(1)} %fusion.4), kind=kOutput, calls=%fused_computation.1 | convolution fusion | flops 2156920832 | bytes 8388608 | tf_op jit(solution)/shard_map/dot_general | solution.py:32
  313.7 0.0 copy-done.2
  313.7 3.8 %add_divide_fusion = f32[512,1024]{1,0:T(8,128)} fusion(f32[512,1024]{1,0:T(8,128)S(1)} %fusion, bf16[2048,512]{0,1:T(8,128)(2,1)S(1)} %fusion.4, bf16[2048,1,1024]{0,2,1:T(8,128)(2,1)S(1)} %copy-done.2), kind=kOutput, calls=%fused_computation.8 | convolution fusion | flops 2149580800 | bytes 10485760 | tf_op jit(solution)/shard_map/dot_general | solution.py:33
Async XLA Ops:
  6.5 96.9 %copy-start = (bf16[128,1024]{1,0:T(8,128)(2,1)S(1)}, bf16[128,1024]{1,0:T(8,128)(2,1)}, u32[]{:S(2)}) copy-start(bf16[128,1024]{1,0:T(8,128)(2,1)} %param.5) | copy-start | bytes 786436
  6.5 99.9 %copy-start.1 = (bf16[512,16]{0,1:T(8,128)(2,1)S(1)}, bf16[512,16]{0,1:T(8,128)(2,1)}, u32[]{:S(2)}) copy-start(bf16[512,16]{0,1:T(8,128)(2,1)} %param.6) | copy-start | bytes 49156
  6.5 96.9 %all-gather.7.cloned.1.call-start = ((), (), s32[]{:S(2)}) async-start(), calls=%async_computation.1 | async-start | bytes 2228224 | tf_op jit(solution)/shard_map/all_gather | solution.py:28
  7.3 191.6 %all-gather.5.cloned.1.call-start = ((), (), s32[]{:S(2)}) async-start(), calls=%async_computation | async-start | bytes 2162688 | tf_op jit(solution)/shard_map/all_gather | solution.py:24
  8.0 301.0 %all-gather.9.cloned.1.call-start = ((), (), s32[]{:S(2)}) async-start(), calls=%async_computation.2 | async-start | bytes 4456448 | tf_op jit(solution)/shard_map/all_gather | solution.py:30
  309.0 4.7 %copy-start.2 = (bf16[2048,1,1024]{0,2,1:T(8,128)(2,1)S(1)}, bf16[2048,1,1024]{0,2,1:T(8,128)(2,1)}, u32[]{:S(2)}) copy-start(bf16[2048,1,1024]{0,2,1:T(8,128)(2,1)} %all-gather.9.cloned.1.call-done) | copy-start | bytes 12582916
Sparse Core Ops, SparseCore 0:
  9.4 93.9 all-gather.6
  106.7 92.0 all-gather.4
  200.9 108.0 all-gather.8
where the time goes:
time: 328 us; the launch traced here: 324 us
  waiting for transfers between devices  249 us (76%)
  blocking collectives  47.3 us (14%)
  matrix products  14.4 us (4%)
  between operations  13.1 us (4%)
    all_gather x1, waiting for transfers between devices, per_device(): piece = lax.all_gather(rot_g, 'rep', axis=0, tiled=True)  107 us
    all_gather x1, waiting for transfers between devices, per_device(): out_cols = lax.all_gather(out_basis, 'rep', axis=1, tiled=True)  95.4 us
    all_gather x1, blocking collectives, per_device(): in_cols = lax.all_gather(in_basis, 'fsdp', axis=1, tiled=True)  47.3 us
    all_gather x1, waiting for transfers between devices, per_device(): lax.all_gather(activations, 'fsdp', axis=0, tiled=True)  45.1 us
  transfers between devices with their start and end apart: 3, of which 3 were waited for; matrix products, arithmetic and copies ran while one was open for 2% of the time, Pallas kernels for 0%

commit v1 on v0

v1 whole, which is shorter than its diff:
```python
import functools

import jax
import jax.numpy as jnp
from jax import lax
from jax.experimental import pallas as pl
from jax.experimental.pallas import tpu as pltpu
from jax.sharding import PartitionSpec as P

MESH = pl.DeviceIdType.MESH
DAMPING = 0.001
TOKENS = 2048
NX, NL, NH, NY = 4, 4, 2, 8
ZROWS = 208
WROWS = 256 - ZROWS
XROWS = 80
NT = (((1,), (1,)), ((), ()))


def dot_nt(a, b):
    return lax.dot_general(a, b, NT, preferred_element_type=jnp.float32)


def square(a):
    wide = a.astype(jnp.float32)
    return (wide * wide).astype(jnp.bfloat16)


def slot_of(x):
    return (x % 2) * 2 + x // 2


def kernel(xb_ref, g_ref, bt_ref, o_ref, xbuf, gbuf, bbuf, rt, bx, rx, sx, send_sem, recv_sem):
    rep, f = lax.axis_index("rep"), lax.axis_index("fsdp")
    x, zl = rep // NL, rep % NL
    zh, y, c = f // 16, (f // 2) % NY, f % 2
    inner = (zl + 1) // 2 % 2 == 1
    xp = (((x + 1) % NX) * NL + zl, f)
    xm = (((x + 3) % NX) * NL + zl, f)
    first = zl + 1 - 2 * (zl % 2)
    nb1 = (x * NL + first, f)
    nb2 = (x * NL + (3 - zl), f)
    yp = (rep, zh * 16 + ((y + 1) % NY) * 2 + c)
    ym = (rep, zh * 16 + ((y + 7) % NY) * 2 + c)
    z4 = (rep, (1 - zh) * 16 + y * 2 + c)
    co = (rep, f + 1 - 2 * c)
    arrivals = (first, 2 - zl // 2, 3 - 3 * (zl // 2))

    sent = []
    ids = [0, 0]

    def new_recv(n=1):
        ids[1] += n
        return ids[1] - n

    def copy(src, dst, s, r, dev):
        return pltpu.make_async_remote_copy(
            src_ref=src, dst_ref=dst, send_sem=send_sem.at[s], recv_sem=recv_sem.at[r],
            device_id=dev, device_id_type=MESH)

    def send(src, dst, r, dev, cond=None):
        s = ids[0]
        ids[0] += 1
        cp = copy(src, dst, s, r, dev)
        if cond is None:
            cp.start()
        else:
            pl.when(cond)(cp.start)
        sent.append((cp, cond))

    def recv(dst, r):
        copy(dst, dst, 0, r, xp).wait_recv()

    barrier = pltpu.get_barrier_semaphore()
    for dev in (xp, xm, nb1, yp, ym, z4, co):
        pl.semaphore_signal(barrier, inc=1, device_id=dev, device_id_type=MESH)

    @pl.when(inner)
    def _():
        pl.semaphore_signal(barrier, inc=1, device_id=nb2, device_id_type=MESH)

    pl.semaphore_wait(barrier, 7 + (zl + 1) // 2 % 2)

    g_own, g_m, g_p, g_2 = (slot_of((x + d) % NX) for d in (0, 3, 1, 2))
    h0, h1 = pl.ds(0, 64), pl.ds(64, 64)
    r_g = new_recv(6)
    send(g_ref.at[h0], gbuf.at[g_own, h0], r_g, xp)
    send(g_ref.at[h1], gbuf.at[g_own, h1], r_g + 1, xm)
    r_b = new_recv(NL)
    send(bt_ref, bbuf.at[zl], r_b + zl, nb1)
    send(bt_ref, bbuf.at[zl], r_b + zl, nb2, inner)
    ys = [((y + d) % NY) % 4 * 2 + ((y + d) % NY) // 4 for d in range(NY)]
    r_zh, r_co = new_recv(), new_recv()
    send(xb_ref, xbuf.at[ys[0], zh, c], r_zh, z4)
    r_y = [[new_recv(2) for _ in range(4)] for _ in range(2)]
    r_c = [[new_recv(2) for _ in range(4)] for _ in range(2)]
    r_co2 = new_recv()
    send(xb_ref, xbuf.at[ys[0], zh, c], r_y[0][0], yp)
    send(xb_ref, xbuf.at[ys[0], zh, c], r_y[0][0] + 1, ym)
    send(xb_ref, xbuf.at[ys[0], zh, c], r_co, co)
    send(g_ref.at[h1], gbuf.at[g_own, h1], r_g + 2, xp)
    send(g_ref.at[h0], gbuf.at[g_own, h0], r_g + 3, xm)

    gbuf[g_own] = g_ref[...]
    bbuf[zl] = bt_ref[...]
    xbuf[ys[0], zh, c] = xb_ref[...]
    left, right = pl.ds(0, 256), pl.ds(256, 256)
    every = pl.ds(0, XROWS)

    def y_step(flow, k):
        hz = zh if flow == 0 else 1 - zh
        for way in range(2):
            src = xbuf.at[ys[(8 - k) % 8 if way == 0 else k], hz, c]
            to = yp if way == 0 else ym
            half = left if way == 0 else right
            r = r_y[flow][k - 1] + way
            if k == 4:
                src = src.at[every, half]
            recv(src, r)
            if k < 3:
                send(src, src, r_y[flow][k] + way, to)
            elif k == 3:
                send(src.at[every, half], src.at[every, half], r_y[flow][k] + way, to)
            send(src, src, r_c[flow][k - 1] + way, co)

    def y_core(flow, k):
        hz = zh if flow == 0 else 1 - zh
        for way in range(2):
            dst = xbuf.at[ys[(8 - k) % 8 if way == 0 else k], hz, 1 - c]
            if k == 4:
                dst = dst.at[every, left if way == 0 else right]
            recv(dst, r_c[flow][k - 1] + way)

    def b_event(e):
        s = arrivals[e]
        recv(bbuf.at[s], r_b + s)
        send(bbuf.at[s], bbuf.at[s], r_b + s, nb2 if e == 0 else nb1, inner)

    y_step(0, 1)
    b_event(0)
    recv(gbuf.at[g_m, h0], r_g)
    send(gbuf.at[g_m, h0], gbuf.at[g_m, h0], r_g + 4, xp)
    recv(gbuf.at[g_p, h1], r_g + 1)
    send(gbuf.at[g_p, h1], gbuf.at[g_p, h1], r_g + 5, xm)
    b_event(1)
    far = xbuf.at[ys[0], 1 - zh, c]
    recv(far, r_zh)
    send(far, far, r_y[1][0], yp)
    send(far, far, r_y[1][0] + 1, ym)
    send(far, far, r_co2, co)
    y_step(0, 2)
    b_event(2)
    y_step(1, 1)
    recv(gbuf.at[g_m, h1], r_g + 2)
    recv(gbuf.at[g_p, h0], r_g + 3)
    recv(gbuf.at[g_2, h0], r_g + 4)
    recv(gbuf.at[g_2, h1], r_g + 5)

    tile = dot_nt(bbuf[...].reshape(256, 1024), gbuf[...].reshape(512, 1024))
    rt[0, zl] = tile.astype(jnp.bfloat16)

    zrows, wrows = pl.ds(0, ZROWS), pl.ds(ZROWS, WROWS)
    r_t = new_recv(NL)
    r_w = new_recv(4)
    r_v = new_recv(NL)
    r_x = [new_recv(6) for _ in range(NL)]

    own = rt.at[0, zl]
    send(own.at[wrows], rt.at[3, zl, wrows], r_w, xp)
    send(own.at[wrows], rt.at[1, zl, wrows], r_w + 1, xm)
    send(own, own, r_t + zl, nb1)
    send(own, own, r_t + zl, nb2, inner)

    def x_sends(s, r):
        for first_half in (True, False):
            lp, lm = (left, right) if first_half else (right, left)
            k = 0 if first_half else 2
            send(rt.at[0, s, zrows, lp], rt.at[3, s, zrows, lp], r + k, xp)
            send(rt.at[0, s, zrows, lm], rt.at[1, s, zrows, lm], r + k + 1, xm)

    def x_forward(s, r):
        recv(rt.at[3, s, zrows, left], r)
        send(rt.at[3, s, zrows, left], rt.at[2, s, zrows, left], r + 4, xp)
        recv(rt.at[1, s, zrows, right], r + 1)
        send(rt.at[1, s, zrows, right], rt.at[2, s, zrows, right], r + 5, xm)

    def t_event(e):
        s = arrivals[e]
        recv(rt.at[0, s], r_t + s)
        send(rt.at[0, s], rt.at[0, s], r_t + s, nb2 if e == 0 else nb1, inner)

    def v_event(e):
        s = arrivals[e]
        part = rt.at[pl.ds(1, 3), s, wrows]
        recv(part, r_v + s)
        send(part, part, r_v + s, nb2 if e == 0 else nb1, inner)

    x_sends(zl, r_x[0])
    y_step(0, 3)
    y_step(1, 2)
    recv(rt.at[3, zl, wrows], r_w)
    send(rt.at[3, zl, wrows, left], rt.at[2, zl, wrows, left], r_w + 2, xp)
    recv(rt.at[1, zl, wrows], r_w + 1)
    send(rt.at[1, zl, wrows, right], rt.at[2, zl, wrows, right], r_w + 3, xm)
    y_step(0, 4)
    t_event(0)
    x_sends(arrivals[0], r_x[1])
    recv(rt.at[2, zl, wrows, left], r_w + 2)
    recv(rt.at[2, zl, wrows, right], r_w + 3)
    mine = rt.at[pl.ds(1, 3), zl, wrows]
    send(mine, mine, r_v + zl, nb1)
    send(mine, mine, r_v + zl, nb2, inner)
    x_forward(zl, r_x[0])
    t_event(1)
    x_sends(arrivals[1], r_x[2])
    y_step(1, 3)
    v_event(0)
    x_forward(arrivals[0], r_x[1])
    t_event(2)
    x_sends(arrivals[2], r_x[3])
    v_event(1)
    y_step(1, 4)
    x_forward(arrivals[1], r_x[2])

    recv(xbuf.at[ys[0], zh, 1 - c], r_co)
    recv(xbuf.at[ys[0], 1 - zh, 1 - c], r_co2)
    for flow in range(2):
        for k in range(1, 5):
            y_core(flow, k)
    for i in range(32):
        ih, iy, ic = i // 16, i // 2 % 8, i % 2
        bx[pl.ds(i * 16, 16), :] = xbuf[iy % 4 * 2 + iy // 4, ih, ic, pl.ds(64, 16), :]

    def rot_x(t, _):
        data = xbuf[pl.ds(t * 2, 2), :, :, pl.ds(0, 64), :].reshape(512, 512)
        turned = dot_nt(bx[...], data).astype(jnp.bfloat16)
        rx[t] = turned
        sx[t] = square(turned)
        return 0

    lax.fori_loop(0, NL, rot_x, 0)
    v_event(2)
    x_forward(arrivals[2], r_x[3])

    def columns(dx):
        col = pl.ds(pl.multiple_of((x + dx) % NX * 256, 256), 256)

        def rows(m, _):
            here = pl.ds(pl.multiple_of(m * 256, 256), 256)
            grad = jnp.zeros((256, 256), jnp.float32)
            scale = jnp.zeros((256, 256), jnp.float32)
            for t in range(NL):
                piece = rt[dx, t]
                grad += dot_nt(rx[t, here, :], piece)
                scale += dot_nt(sx[t, here, :], square(piece))
            o_ref[here, col] = (grad / TOKENS) / (scale / TOKENS + DAMPING)
            return 0

        lax.fori_loop(0, 2, rows, 0)

    slots = (zl,) + arrivals
    columns(0)
    for i in range(NL):
        recv(rt.at[1, slots[i], zrows, left], r_x[i] + 3)
    columns(1)
    for i in range(NL):
        recv(rt.at[3, slots[i], zrows, right], r_x[i] + 2)
    columns(3)
    for i in range(NL):
        recv(rt.at[2, slots[i], zrows, left], r_x[i] + 4)
        recv(rt.at[2, slots[i], zrows, right], r_x[i] + 5)
    columns(2)

    for cp, cond in sent:
        if cond is None:
            cp.wait_send()
        else:
            pl.when(cond)(cp.wait_send)


def per_device(activations, out_grads, in_basis, out_basis):
    xb = jnp.concatenate([activations, in_basis.T], axis=0)
    bf = jnp.bfloat16
    vmem = pl.BlockSpec(memory_space=pltpu.VMEM)
    return pl.pallas_call(
        kernel,
        out_shape=jax.ShapeDtypeStruct((512, 1024), jnp.float32),
        in_specs=[vmem] * 3,
        out_specs=vmem,
        scratch_shapes=[
            pltpu.VMEM((NY, NH, 2, XROWS, 512), bf),
            pltpu.VMEM((NX, 128, 1024), bf),
            pltpu.VMEM((NL, 64, 1024), bf),
            pltpu.VMEM((NX, NL, 256, 512), bf),
            pltpu.VMEM((512, 512), bf),
            pltpu.VMEM((NL, 512, 512), bf),
            pltpu.VMEM((NL, 512, 512), bf),
            pltpu.SemaphoreType.DMA((100,)),
            pltpu.SemaphoreType.DMA((100,)),
        ],
        compiler_params=pltpu.CompilerParams(
            collective_id=0, has_side_effects=True, vmem_limit_bytes=48 * 2**20),
        cost_estimate=pl.CostEstimate(
            flops=6 * 10**9, bytes_accessed=4 * 2**20, transcendentals=0),
        name="gather_and_scale",
    )(xb, out_grads, out_basis.T)


def solution(mesh):
    in_specs = (P("fsdp", "rep"), P("rep", "fsdp"), P("rep", "fsdp"), P("fsdp", "rep"))
    out_specs = P("rep", "fsdp")
    return jax.shard_map(
        per_device, mesh=mesh, in_specs=in_specs, out_specs=out_specs, check_vma=False
    )
```

time: 328 us -> 68.4 us (0.21)
  waiting for transfers between devices: 249 us -> 0 us
  Pallas kernels: 0 us -> 63 us
  blocking collectives: 47.3 us -> 0 us
  matrix products: 14.4 us -> 0 us
  between operations: 13.1 us -> 0.01 us
    all_gather x3 -> x0, waiting for transfers between devices: 248 us -> none  [the longest x1 107 us: per_device(): piece = lax.all_gather(rot_g, 'rep', axis=0, tiled=True)]
    pallas_call x0 -> x1, Pallas kernels: none -> 63 us  [per_device(): pl.pallas_call(kernel, out_shape=jax.ShapeDtypeStruct((512, 1024), jnp.fl...]
    all_gather x1 -> x0, blocking collectives: 47.3 us -> none  [per_device(): in_cols = lax.all_gather(in_basis, 'fsdp', axis=1, tiled=True)]
    dot_general x4 -> x0, matrix products: 14.4 us -> none  [the longest x2 5.87 us: rotate(): jnp.einsum('tkb,kbc->tkc', parts, blocks, preferred_element_type=jnp.floa...]
  transfers between devices with their start and end apart: 3 -> 0, of which waited for: 3 -> 0; matrix products, arithmetic and copies ran while one was open for 2% -> 0% of each run, Pallas kernels for 0% -> 0%
where the time goes in v1:
time: 68.4 us; the launch traced here: 67.1 us
  Pallas kernels  63 us (92%)
  local copies, waits for them, and re-layouts  3.17 us (5%)
  other arithmetic  0.86 us (1%)
    pallas_call x1, Pallas kernels, per_device(): pl.pallas_call(kernel, out_shape=jax.ShapeDtypeStruct((512, 1024), jnp.fl...  63 us
    unnamed x5, local copies, waits for them, and re-layouts  3.17 us

profile of v1, /device:TPU:56, one launch (start us, length us, event | category | flops | bytes accessed | tf_op | source)
XLA Modules:
  0.0 67.1 jit_solution(17111320407726751311)
XLA Ops:
  0.0 0.9 %pad_maximum_fusion.xb_ref = bf16[80,512]{1,0:T(8,128)(2,1)S(1)} fusion(bf16[16,512]{1,0:T(8,128)(2,1)} %bitcast.3, bf16[64,512]{1,0:T(8,128)(2,1)} %param.4), kind=kLoop, calls=%fused_computation | loop fusion | flops 163840 | bytes 163840 | tf_op jit(solution)/shard_map/concatenate | solution.py:282
  0.9 0.0 copy-start
  0.9 0.9 %copy-done = bf16[128,1024]{1,0:T(8,128)(2,1)S(1)} copy-done((bf16[128,1024]{1,0:T(8,128)(2,1)S(1)}, bf16[128,1024]{1,0:T(8,128)(2,1)}, u32[]{:S(2)}) %copy-start) | copy-done | bytes 262168
  1.8 0.0 copy-start.1
  1.8 0.9 %copy-done.1 = bf16[1024,64]{0,1:T(8,128)(2,1)S(1)} copy-done((bf16[1024,64]{0,1:T(8,128)(2,1)S(1)}, bf16[1024,64]{0,1:T(8,128)(2,1)}, u32[]{:S(2)}) %copy-start.1) | copy-done | bytes 131096
  2.7 63.0 %gather_and_scale.1 = f32[512,1024]{1,0:T(8,128)S(1)} custom-call(bf16[80,512]{1,0:T(8,128)(2,1)S(1)} %pad_maximum_fusion.xb_ref, bf16[128,1024]{1,0:T(8,128)(2,1)S(1)} %copy-done, bf16[64,1024]{1,0:T(8,128)(2,1)S(1)} %bitcast.2), custom_call_target="tpu_custom_call" | custom-call | flops 6000000000 | bytes 4194304 | tf_op jit(solution)/shard_map/gather_and_scale/pallas_call | solution.py:285
  65.8 1.3 %copy.6 = f32[512,1024]{1,0:T(8,128)} copy(f32[512,1024]{1,0:T(8,128)S(1)} %gather_and_scale.1) | data formatting | bytes 4194304
Async XLA Ops:
  0.9 0.9 %copy-start = (bf16[128,1024]{1,0:T(8,128)(2,1)S(1)}, bf16[128,1024]{1,0:T(8,128)(2,1)}, u32[]{:S(2)}) copy-start(bf16[128,1024]{1,0:T(8,128)(2,1)} %g_ref.1) | copy-start | bytes 786436
  1.8 0.9 %copy-start.1 = (bf16[1024,64]{0,1:T(8,128)(2,1)S(1)}, bf16[1024,64]{0,1:T(8,128)(2,1)}, u32[]{:S(2)}) copy-start(bf16[1024,64]{0,1:T(8,128)(2,1)} %param.7) | copy-start | bytes 393220

commit v2 on v1

v2 whole, which is shorter than its diff:
```python
import functools

import jax
import jax.numpy as jnp
from jax import lax
from jax.experimental import pallas as pl
from jax.experimental.pallas import tpu as pltpu
from jax.sharding import PartitionSpec as P

MESH = pl.DeviceIdType.MESH
DAMPING = 0.001
TOKENS = 2048
NX, NL, NH, NY = 4, 4, 2, 8
ZROWS = 208
WROWS = 256 - ZROWS
XROWS = 80
NT = (((1,), (1,)), ((), ()))


def dot_nt(a, b):
    return lax.dot_general(a, b, NT, preferred_element_type=jnp.float32)


def square(a):
    wide = a.astype(jnp.float32)
    return (wide * wide).astype(jnp.bfloat16)


def slot_of(x):
    return (x % 2) * 2 + x // 2


def kernel(x_ref, i_ref, g_ref, bt_ref, o_ref, xbuf, gbuf, bbuf, rt, bx, rx, sx, send_sem, recv_sem, own_sem):
    rep, f = lax.axis_index("rep"), lax.axis_index("fsdp")
    x, zl = rep // NL, rep % NL
    zh, y, c = f // 16, (f // 2) % NY, f % 2
    inner = (zl + 1) // 2 % 2 == 1
    xp = (((x + 1) % NX) * NL + zl, f)
    xm = (((x + 3) % NX) * NL + zl, f)
    x2 = (((x + 2) % NX) * NL + zl, f)
    first = zl + 1 - 2 * (zl % 2)
    arrivals = (first, 2 - zl // 2, 3 - 3 * (zl // 2))
    line = [(x * NL + s, f) for s in arrivals]
    nb1 = line[0]
    nb2 = (x * NL + (3 - zl), f)
    yd = [(rep, zh * 16 + ((y + d) % NY) * 2 + c) for d in range(NY)]
    z4 = (rep, (1 - zh) * 16 + y * 2 + c)
    co = (rep, f + 1 - 2 * c)

    sent = []
    ids = [0, 0]

    def new_recv(n=1):
        ids[1] += n
        return ids[1] - n

    def copy(src, dst, s, r, dev):
        return pltpu.make_async_remote_copy(
            src_ref=src, dst_ref=dst, send_sem=send_sem.at[s], recv_sem=recv_sem.at[r],
            device_id=dev, device_id_type=MESH)

    def send(src, dst, r, dev, cond=None):
        s = ids[0]
        ids[0] += 1
        cp = copy(src, dst, s, r, dev)
        if cond is None:
            cp.start()
        else:
            pl.when(cond)(cp.start)
        sent.append((cp, cond))

    def pass_on(ref, r, dev, cond=None):
        send(ref, ref, r, dev, cond)

    def recv(dst, r):
        copy(dst, dst, 0, r, xp).wait_recv()

    barrier = pltpu.get_barrier_semaphore()
    partners = [xp, xm, x2, *line, yd[1], yd[7], yd[2], yd[6], z4, co]
    for dev in partners:
        pl.semaphore_signal(barrier, inc=1, device_id=dev, device_id_type=MESH)

    ys = [((y + d) % NY) % 4 * 2 + ((y + d) % NY) // 4 for d in range(NY)]
    g_own, g_m, g_p, g_2 = (slot_of((x + d) % NX) for d in (0, 3, 1, 2))
    x_own = xbuf.at[ys[0], zh, c]
    load = [
        pltpu.make_async_copy(g_ref, gbuf.at[g_own], own_sem.at[0]),
        pltpu.make_async_copy(bt_ref, bbuf.at[zl], own_sem.at[1]),
        pltpu.make_async_copy(x_ref, x_own.at[pl.ds(0, 64)], own_sem.at[2]),
        pltpu.make_async_copy(i_ref, x_own.at[pl.ds(64, 16)], own_sem.at[3]),
    ]
    for cp in load:
        cp.start()
    for cp in load:
        cp.wait()
    pl.semaphore_wait(barrier, len(partners))

    left, right = pl.ds(0, 256), pl.ds(256, 256)
    h0, h1 = pl.ds(0, 64), pl.ds(64, 64)
    every = pl.ds(0, XROWS)

    r_g = new_recv(6)
    pass_on(gbuf.at[g_own, h0], r_g, xp)
    pass_on(gbuf.at[g_own, h1], r_g + 1, xm)
    r_b = new_recv(NL)
    for dev in line:
        pass_on(bbuf.at[zl], r_b + zl, dev)
    pass_on(gbuf.at[g_own, h1], r_g + 2, xp)
    pass_on(gbuf.at[g_own, h0], r_g + 3, xm)
    r_zh = new_recv()
    pass_on(x_own, r_zh, z4)
    r_near = [[new_recv() for _ in range(4)] for _ in range(2)]
    near = (1, 7, 2, 6)

    def x_near(flow):
        piece = xbuf.at[ys[0], zh if flow == 0 else 1 - zh, c]
        for k, d in enumerate(near):
            pass_on(piece, r_near[flow][k], yd[d])

    x_near(0)

    recv(gbuf.at[g_m, h0], r_g)
    pass_on(gbuf.at[g_m, h0], r_g + 4, xp)
    recv(gbuf.at[g_p, h1], r_g + 1)
    pass_on(gbuf.at[g_p, h1], r_g + 5, xm)
    recv(xbuf.at[ys[0], 1 - zh, c], r_zh)
    x_near(1)
    r_core = [new_recv() for _ in range(9)]
    pass_on(xbuf.at[ys[0], :, c], r_core[0], co)
    recv(gbuf.at[g_m, h1], r_g + 2)
    recv(gbuf.at[g_p, h0], r_g + 3)
    recv(gbuf.at[g_2, h0], r_g + 4)
    recv(gbuf.at[g_2, h1], r_g + 5)
    for s in arrivals:
        recv(bbuf.at[s], r_b + s)

    tile = dot_nt(bbuf[...].reshape(256, 1024), gbuf[...].reshape(512, 1024))
    rt[0, zl] = tile.astype(jnp.bfloat16)

    zrows, wrows = pl.ds(0, ZROWS), pl.ds(ZROWS, WROWS)
    r_t = new_recv(NL)
    r_w = new_recv(3)
    r_v = new_recv(NL)
    r_x = [new_recv(6) for _ in range(NL)]

    def x_sends(s, r, first_half):
        lp, lm = (left, right) if first_half else (right, left)
        k = 0 if first_half else 2
        send(rt.at[0, s, zrows, lp], rt.at[3, s, zrows, lp], r + k, xp)
        send(rt.at[0, s, zrows, lm], rt.at[1, s, zrows, lm], r + k + 1, xm)

    def x_forward(s, r):
        recv(rt.at[3, s, zrows, left], r)
        send(rt.at[3, s, zrows, left], rt.at[2, s, zrows, left], r + 4, xp)
        recv(rt.at[1, s, zrows, right], r + 1)
        send(rt.at[1, s, zrows, right], rt.at[2, s, zrows, right], r + 5, xm)

    def t_event(e):
        s = arrivals[e]
        recv(rt.at[0, s], r_t + s)
        pass_on(rt.at[0, s], r_t + s, nb2 if e == 0 else nb1, inner)
        x_sends(s, r_x[e + 1], True)
        x_sends(s, r_x[e + 1], False)

    own = rt.at[0, zl]
    x_sends(zl, r_x[0], True)
    pass_on(own, r_t + zl, nb1)
    pass_on(own, r_t + zl, nb2, inner)
    x_sends(zl, r_x[0], False)
    send(own.at[wrows], rt.at[3, zl, wrows], r_w, xp)
    send(own.at[wrows], rt.at[1, zl, wrows], r_w + 1, xm)
    send(own.at[wrows], rt.at[2, zl, wrows], r_w + 2, x2)

    x_forward(zl, r_x[0])
    r_far = [new_recv() for _ in range(4)]
    for flow in range(2):
        hz = zh if flow == 0 else 1 - zh
        for k, d in enumerate(near):
            recv(xbuf.at[ys[(8 - d) % 8], hz, c], r_near[flow][k])
    for way in range(2):
        piece = xbuf.at[ys[6 if way == 0 else 2], :, c]
        pass_on(piece, r_far[way], yd[1 if way == 0 else 7])
        half = xbuf.at[ys[6 if way == 0 else 2], way, c]
        pass_on(half, r_far[2 + way], yd[2 if way == 0 else 6])
    for k, d in enumerate(near):
        pass_on(xbuf.at[ys[d], :, c], r_core[1 + k], co)

    t_event(0)
    for d, slot in enumerate((3, 1, 2)):
        recv(rt.at[slot, zl, wrows], r_w + d)
    mine = rt.at[pl.ds(1, 3), zl, wrows]
    for dev in line:
        pass_on(mine, r_v + zl, dev)
    x_forward(arrivals[0], r_x[1])
    t_event(1)
    x_forward(arrivals[1], r_x[2])
    for way in range(2):
        recv(xbuf.at[ys[5 if way == 0 else 3], :, c], r_far[way])
        recv(xbuf.at[ys[4], way, c], r_far[2 + way])
    for k, d in enumerate((3, 5, 4)):
        pass_on(xbuf.at[ys[d], :, c], r_core[5 + k], co)
    t_event(2)

    for k, d in enumerate((0,) + near + (3, 5, 4)):
        recv(xbuf.at[ys[d], :, 1 - c], r_core[k])
    for i in range(32):
        ih, iy, ic = i // 16, i // 2 % 8, i % 2
        bx[pl.ds(i * 16, 16), :] = xbuf[iy % 4 * 2 + iy // 4, ih, ic, pl.ds(64, 16), :]

    def rot_x(t, _):
        data = xbuf[pl.ds(t * 2, 2), :, :, pl.ds(0, 64), :].reshape(512, 512)
        turned = dot_nt(bx[...], data).astype(jnp.bfloat16)
        rx[t] = turned
        sx[t] = square(turned)
        return 0

    lax.fori_loop(0, NL, rot_x, 0)
    x_forward(arrivals[2], r_x[3])

    def columns(dx):
        col = pl.ds(pl.multiple_of((x + dx) % NX * 256, 256), 256)

        def rows(m, _):
            here = pl.ds(pl.multiple_of(m * 256, 256), 256)
            grad = jnp.zeros((256, 256), jnp.float32)
            scale = jnp.zeros((256, 256), jnp.float32)
            for t in range(NL):
                piece = rt[dx, t]
                grad += dot_nt(rx[t, here, :], piece)
                scale += dot_nt(sx[t, here, :], square(piece))
            o_ref[here, col] = (grad / TOKENS) / (scale / TOKENS + DAMPING)
            return 0

        lax.fori_loop(0, 2, rows, 0)

    slots = (zl,) + arrivals
    columns(0)
    for s in arrivals:
        recv(rt.at[pl.ds(1, 3), s, wrows], r_v + s)
    for i in range(NL):
        recv(rt.at[1, slots[i], zrows, left], r_x[i] + 3)
    columns(1)
    for i in range(NL):
        recv(rt.at[3, slots[i], zrows, right], r_x[i] + 2)
    columns(3)
    for i in range(NL):
        recv(rt.at[2, slots[i], zrows, left], r_x[i] + 4)
        recv(rt.at[2, slots[i], zrows, right], r_x[i] + 5)
    columns(2)

    for cp, cond in sent:
        if cond is None:
            cp.wait_send()
        else:
            pl.when(cond)(cp.wait_send)


def per_device(activations, out_grads, in_basis, out_basis):
    bf = jnp.bfloat16
    vmem = pl.BlockSpec(memory_space=pltpu.VMEM)
    return pl.pallas_call(
        kernel,
        out_shape=jax.ShapeDtypeStruct((512, 1024), jnp.float32),
        in_specs=[pl.BlockSpec(memory_space=pltpu.HBM)] * 4,
        out_specs=vmem,
        scratch_shapes=[
            pltpu.VMEM((NY, NH, 2, XROWS, 512), bf),
            pltpu.VMEM((NX, 128, 1024), bf),
            pltpu.VMEM((NL, 64, 1024), bf),
            pltpu.VMEM((NX, NL, 256, 512), bf),
            pltpu.VMEM((512, 512), bf),
            pltpu.VMEM((NL, 512, 512), bf),
            pltpu.VMEM((NL, 512, 512), bf),
            pltpu.SemaphoreType.DMA((100,)),
            pltpu.SemaphoreType.DMA((100,)),
            pltpu.SemaphoreType.DMA((4,)),
        ],
        compiler_params=pltpu.CompilerParams(
            collective_id=0, has_side_effects=True, vmem_limit_bytes=48 * 2**20),
        cost_estimate=pl.CostEstimate(
            flops=6 * 10**9, bytes_accessed=4 * 2**20, transcendentals=0),
        name="gather_and_scale",
    )(activations, in_basis.T, out_grads, out_basis.T)


def solution(mesh):
    in_specs = (P("fsdp", "rep"), P("rep", "fsdp"), P("rep", "fsdp"), P("fsdp", "rep"))
    out_specs = P("rep", "fsdp")
    return jax.shard_map(
        per_device, mesh=mesh, in_specs=in_specs, out_specs=out_specs, check_vma=False
    )
```

time: 68.4 us -> 76.9 us (1.12); the launches traced: 67.1 us -> 76.4 us
  Pallas kernels: 63 us -> 71.6 us
  local copies, waits for them, and re-layouts: 3.17 us -> 4.73 us
  other arithmetic: 0.86 us -> 0 us
    pallas_call x1, Pallas kernels: 63 us -> 71.6 us  [per_device(): pl.pallas_call(kernel, out_shape=jax.ShapeDtypeStruct((512, 1024), jnp.fl...]
    unnamed x5 -> x9, local copies, waits for them, and re-layouts: 3.17 us -> 4.73 us
    concatenate x1 -> x0, other arithmetic: 0.86 us -> none  [per_device(): xb = jnp.concatenate([activations, in_basis.T], axis=0)]
where the time goes in v2:
time: 76.9 us; the launch traced here: 76.4 us
  Pallas kernels  71.6 us (93%)
  local copies, waits for them, and re-layouts  4.73 us (6%)
    pallas_call x1, Pallas kernels, per_device(): pl.pallas_call(kernel, out_shape=jax.ShapeDtypeStruct((512, 1024), jnp.fl...  71.6 us
    unnamed x9, local copies, waits for them, and re-layouts  4.73 us

profile of v2, /device:TPU:56, one launch (start us, length us, event | category | flops | bytes accessed | tf_op | source)
XLA Modules:
  0.0 76.4 jit_solution(2174389493991515038)
XLA Ops:
  0.0 0.0 copy-start
  0.0 0.9 %copy-done = bf16[128,1024]{1,0:T(8,128)(2,1)S(1)} copy-done((bf16[128,1024]{1,0:T(8,128)(2,1)S(1)}, bf16[128,1024]{1,0:T(8,128)(2,1)}, u32[]{:S(2)}) %copy-start) | copy-done | bytes 262168
  1.0 0.0 copy-start.1
  1.0 0.9 %copy-done.1 = bf16[1024,64]{0,1:T(8,128)(2,1)S(1)} copy-done((bf16[1024,64]{0,1:T(8,128)(2,1)S(1)}, bf16[1024,64]{0,1:T(8,128)(2,1)}, u32[]{:S(2)}) %copy-start.1) | copy-done | bytes 131096
  1.9 0.0 copy-start.2
  1.9 0.8 %copy-done.2 = bf16[64,512]{1,0:T(8,128)(2,1)S(1)} copy-done((bf16[64,512]{1,0:T(8,128)(2,1)S(1)}, bf16[64,512]{1,0:T(8,128)(2,1)}, u32[]{:S(2)}) %copy-start.2) | copy-done | bytes 65560
  2.7 0.0 copy-start.3
  2.7 0.7 copy-done.3
  3.4 71.6 %gather_and_scale.1 = f32[512,1024]{1,0:T(8,128)S(1)} custom-call(bf16[64,512]{1,0:T(8,128)(2,1)S(1)} %copy-done.2, bf16[16,512]{1,0:T(8,128)(2,1)S(1)} %bitcast.3, bf16[128,1024]{1,0:T(8,128)(2,1)S(1)} %copy-done, bf16[64,1024]{1,0:T(8,128)(2,1)S(1)} %bitcast.2), custom_call_target="tpu_custom_call" | custom-call | flops 6000000000 | bytes 4194304 | tf_op jit(solution)/shard_map/gather_and_scale/pallas_call | solution.py:261
  75.1 1.3 %copy.6 = f32[512,1024]{1,0:T(8,128)} copy(f32[512,1024]{1,0:T(8,128)S(1)} %gather_and_scale.1) | data formatting | bytes 4194304
Async XLA Ops:
  0.0 0.9 %copy-start = (bf16[128,1024]{1,0:T(8,128)(2,1)S(1)}, bf16[128,1024]{1,0:T(8,128)(2,1)}, u32[]{:S(2)}) copy-start(bf16[128,1024]{1,0:T(8,128)(2,1)} %g_ref.1) | copy-start | bytes 786436
  1.0 0.9 %copy-start.1 = (bf16[1024,64]{0,1:T(8,128)(2,1)S(1)}, bf16[1024,64]{0,1:T(8,128)(2,1)}, u32[]{:S(2)}) copy-start(bf16[1024,64]{0,1:T(8,128)(2,1)} %param.7) | copy-start | bytes 393220
  1.9 0.8 %copy-start.2 = (bf16[64,512]{1,0:T(8,128)(2,1)S(1)}, bf16[64,512]{1,0:T(8,128)(2,1)}, u32[]{:S(2)}) copy-start(bf16[64,512]{1,0:T(8,128)(2,1)} %x_ref.1) | copy-start | bytes 196612
  2.7 0.7 copy-start.3

commit v3 on v0

v3 whole, which is shorter than its diff:
```python
import functools

import jax
import jax.numpy as jnp
from jax import lax
from jax.experimental import pallas as pl
from jax.experimental.pallas import tpu as pltpu
from jax.sharding import PartitionSpec as P

MESH = pl.DeviceIdType.MESH
DAMPING = 0.001
TOKENS = 2048
NX, NL, NH, NY = 4, 4, 2, 8
XROWS = 80
WROWS = 32
A_ROWS = pl.ds(0, 128)
B_ROWS = pl.ds(128, 128)
BZ_ROWS = pl.ds(128, 128 - WROWS)
W_ROWS = pl.ds(256 - WROWS, WROWS)
LEFT, RIGHT = pl.ds(0, 256), pl.ds(256, 256)
NT = (((1,), (1,)), ((), ()))
END_ORDER = (
    "Z4", "B0", "G2", "Y01", "G1", "GA", "XZ", "B1", "B2", "GB", "Y02", "WX", "Y11", "T0A",
    "WF", "T0B", "Y12", "Y03", "T1A", "F1A", "WZ", "F0B", "T1B", "Y04", "F0A", "Y13", "T2A",
    "Y14", "T2B", "F1B", "RX", "V1", "F2B", "V0", "V2", "F2A", "C0", "F3B", "F3A",
)
INNER_ORDER = (
    "B1", "B0", "G1", "G2", "Z4", "Y01", "B2", "GA", "GB", "Y02", "XZ", "WX", "T0A", "T1A",
    "Y03", "WF", "Y11", "T1B", "T0B", "T2A", "F1A", "F0B", "Y12", "Y04", "T2B", "WZ", "V0",
    "Y13", "F0A", "V1", "F1B", "F2B", "Y14", "F2A", "F3A", "V2", "RX", "F3B", "C0",
)


def dot_nt(a, b):
    return lax.dot_general(a, b, NT, preferred_element_type=jnp.float32)


def square(a):
    wide = a.astype(jnp.float32)
    return (wide * wide).astype(jnp.bfloat16)


def slot_of(x):
    return (x % 2) * 2 + x // 2


def along_plus(i, h):
    return (h + i) % 2 == 0


def kernel(x_ref, i_ref, g_ref, bt_ref, o_ref, out, xbuf, gbuf, bbuf, rt, bx, rx, sx, send_sem, recv_sem, own_sem, out_sem):
    rep, f = lax.axis_index("rep"), lax.axis_index("fsdp")
    x, zl = rep // NL, rep % NL
    zh, y, c = f // 16, (f // 2) % NY, f % 2
    inner = (zl + 1) // 2 % 2
    xp = (((x + 1) % NX) * NL + zl, f)
    xm = (((x + 3) % NX) * NL + zl, f)
    arrivals = (zl + 1 - 2 * (zl % 2), 2 - zl // 2, 3 - 3 * (zl // 2))
    slots = (zl,) + arrivals
    nb1 = (x * NL + arrivals[0], f)
    nb2 = (x * NL + (3 - zl), f)
    yp = (rep, zh * 16 + ((y + 1) % NY) * 2 + c)
    ym = (rep, zh * 16 + ((y + 7) % NY) * 2 + c)
    z4 = (rep, (1 - zh) * 16 + y * 2 + c)
    co = (rep, f + 1 - 2 * c)
    ys = [((y + d) % NY) % 4 * 2 + ((y + d) % NY) // 4 for d in range(NY)]
    g_own, g_m, g_p, g_2 = (slot_of((x + d) % NX) for d in (0, 3, 1, 2))
    pair = zl // 2 * 2
    hzs = (zh, 1 - zh)

    count = [0]

    def sems(n):
        count[0] += n
        return count[0] - n

    r_g, r_b, r_zh = sems(6), sems(2 * NL), sems(1)
    r_y, r_c, r_co = sems(16), sems(16), sems(2)
    r_t, r_x, r_f = sems(2 * NL), sems(4 * NL), sems(2 * NL)
    r_w, r_v = sems(4), sems(NL)

    def copy(src, dst, s, r, dev):
        return pltpu.make_async_remote_copy(
            src_ref=src, dst_ref=dst, send_sem=send_sem.at[s], recv_sem=recv_sem.at[r],
            device_id=dev, device_id_type=MESH)

    def arrived(dst, r):
        copy(dst, dst, 0, r, xp).wait_recv()

    barrier = pltpu.get_barrier_semaphore()
    for dev in (xp, xm, nb1, yp, ym, z4, co):
        pl.semaphore_signal(barrier, inc=1, device_id=dev, device_id_type=MESH)

    @pl.when(inner == 1)
    def _():
        pl.semaphore_signal(barrier, inc=1, device_id=nb2, device_id_type=MESH)

    x_own = xbuf.at[ys[0], zh, c]
    load = [
        pltpu.make_async_copy(g_ref, gbuf.at[g_own], own_sem.at[0]),
        pltpu.make_async_copy(bt_ref, bbuf.at[zl], own_sem.at[1]),
        pltpu.make_async_copy(x_ref, x_own.at[pl.ds(0, 64)], own_sem.at[2]),
        pltpu.make_async_copy(i_ref, x_own.at[pl.ds(64, 16)], own_sem.at[3]),
    ]
    for cp in load:
        cp.start()
    for cp in load:
        cp.wait()
    pl.semaphore_wait(barrier, 7 + inner)

    def rot_x(t, _):
        data = xbuf[pl.ds(t * 2, 2), :, :, pl.ds(0, 64), :].reshape(512, 512)
        turned = dot_nt(bx[...], data).astype(jnp.bfloat16)
        rx[t] = turned
        sx[t] = square(turned)
        return 0

    def columns(dx):
        col = pl.ds(pl.multiple_of((x + dx) % NX * 256, 256), 256)

        def rows(m, _):
            here = pl.ds(pl.multiple_of(m * 256, 256), 256)
            grad = jnp.zeros((256, 256), jnp.float32)
            scale = jnp.zeros((256, 256), jnp.float32)
            for t in range(NL):
                halves = [rt[dx, t, A_ROWS, :], rt[dx, t, B_ROWS, :]]
                piece = jnp.concatenate(halves if t < 2 else halves[::-1], axis=0)
                grad += dot_nt(rx[t, here, :], piece)
                scale += dot_nt(sx[t, here, :], square(piece))
            out[here, col] = (grad / TOKENS) / (scale / TOKENS + DAMPING)
            return 0

        lax.fori_loop(0, 2, rows, 0)
        return pltpu.make_async_copy(out.at[:, col], o_ref.at[:, col], out_sem.at[dx])

    def program(inside, order, finish):
        count = [0]

        def send(src, dst, r, dev):
            cp = copy(src, dst, count[0], r, dev)
            count[0] += 1
            if finish:
                cp.wait_send()
            else:
                cp.start()

        def recv(dst, r):
            if not finish:
                arrived(dst, r)

        def pass_on(ref, r, dev):
            send(ref, ref, r, dev)

        def own_z(ref, r):
            pass_on(ref, r, nb1)
            if inside:
                pass_on(ref, r, nb2)

        def next_z(e, ref, r):
            if inside:
                pass_on(ref, r, nb2 if e == 0 else nb1)

        def b_part(s, q):
            return bbuf.at[s, :, pl.ds(q * 512, 512)]

        def x_sends(i, h):
            s, r = slots[i], r_x + 4 * i + 2 * h
            rows = BZ_ROWS if h else A_ROWS
            send(rt.at[0, s, rows], rt.at[3, s, rows], r, xp)
            send(rt.at[0, s, rows], rt.at[1, s, rows], r + 1, xm)

        def tile(h):
            first = pair if h == 0 else 2 - pair
            rows = B_ROWS if h else A_ROWS
            if not finish:
                basis = bbuf[pl.ds(first, 2)].reshape(128, 1024)
                turned = dot_nt(basis, gbuf[...].reshape(512, 1024))
                rt[0, zl, rows, :] = turned.astype(jnp.bfloat16)
            own_z(rt.at[0, zl, rows], r_t + 2 * zl + h)
            x_sends(0, h)

        def y_event(flow, k):
            for way in range(2):
                src = xbuf.at[ys[(8 - k) % 8 if way == 0 else k], hzs[flow], c]
                to = yp if way == 0 else ym
                half = src.at[pl.ds(0, XROWS), LEFT if way == 0 else RIGHT]
                if k == 4:
                    src = half
                r = (flow * 4 + k - 1) * 2 + way
                recv(src, r_y + r)
                if k < 3:
                    pass_on(src, r_y + r + 2, to)
                elif k == 3:
                    pass_on(half, r_y + r + 2, to)
                pass_on(src, r_c + r, co)

        def event(name):
            kind = name[0]
            if name == "Z4":
                pass_on(x_own, r_zh, z4)
            elif name == "XZ":
                far = xbuf.at[ys[0], 1 - zh, c]
                recv(far, r_zh)
                pass_on(far, r_y + 8, yp)
                pass_on(far, r_y + 9, ym)
                pass_on(far, r_co + 1, co)
            elif kind == "Y":
                y_event(int(name[1]), int(name[2]))
            elif kind == "B":
                e = int(name[1])
                s = arrivals[e]
                for q in range(2):
                    recv(b_part(s, q), r_b + 2 * s + q)
                    next_z(e, b_part(s, q), r_b + 2 * s + q)
            elif name == "G1":
                recv(gbuf.at[g_m, h0], r_g)
                pass_on(gbuf.at[g_m, h0], r_g + 4, xp)
            elif name == "G2":
                recv(gbuf.at[g_p, h1], r_g + 1)
                pass_on(gbuf.at[g_p, h1], r_g + 5, xm)
            elif name == "GA":
                recv(gbuf.at[g_m, h1], r_g + 2)
                recv(gbuf.at[g_p, h0], r_g + 3)
                recv(gbuf.at[g_2, h0], r_g + 4)
                recv(gbuf.at[g_2, h1], r_g + 5)
                tile(0)
            elif name == "GB":
                tile(1)
            elif name == "WX":
                send(rt.at[0, zl, W_ROWS], rt.at[3, zl, W_ROWS], r_w, xp)
                send(rt.at[0, zl, W_ROWS], rt.at[1, zl, W_ROWS], r_w + 1, xm)
            elif name == "WF":
                recv(rt.at[3, zl, W_ROWS], r_w)
                send(rt.at[3, zl, W_ROWS, LEFT], rt.at[2, zl, W_ROWS, LEFT], r_w + 2, xp)
                recv(rt.at[1, zl, W_ROWS], r_w + 1)
                send(rt.at[1, zl, W_ROWS, RIGHT], rt.at[2, zl, W_ROWS, RIGHT], r_w + 3, xm)
            elif name == "WZ":
                recv(rt.at[2, zl, W_ROWS, LEFT], r_w + 2)
                recv(rt.at[2, zl, W_ROWS, RIGHT], r_w + 3)
                own_z(rt.at[pl.ds(1, 3), zl, W_ROWS], r_v + zl)
            elif kind == "V":
                e = int(name[1])
                s = arrivals[e]
                part = rt.at[pl.ds(1, 3), s, W_ROWS]
                recv(part, r_v + s)
                next_z(e, part, r_v + s)
            elif kind == "T":
                e, h = int(name[1]), "AB".index(name[2])
                s = arrivals[e]
                part = rt.at[0, s, B_ROWS if h else A_ROWS]
                recv(part, r_t + 2 * s + h)
                next_z(e, part, r_t + 2 * s + h)
                x_sends(e + 1, h)
            elif kind == "F":
                i, h = int(name[1]), "AB".index(name[2])
                s, rows, r = slots[i], BZ_ROWS if h else A_ROWS, r_x + 4 * i + 2 * h
                if along_plus(i, h):
                    recv(rt.at[3, s, rows], r)
                    send(rt.at[3, s, rows], rt.at[2, s, rows], r_f + 2 * i + h, xp)
                else:
                    recv(rt.at[1, s, rows], r + 1)
                    send(rt.at[1, s, rows], rt.at[2, s, rows], r_f + 2 * i + h, xm)
            elif finish:
                pass
            elif name == "RX":
                for flow in range(2):
                    recv(xbuf.at[ys[0], hzs[flow], 1 - c], r_co + flow)
                    for k in range(1, 5):
                        for way in range(2):
                            dst = xbuf.at[ys[(8 - k) % 8 if way == 0 else k], hzs[flow], 1 - c]
                            if k == 4:
                                dst = dst.at[pl.ds(0, XROWS), LEFT if way == 0 else RIGHT]
                            recv(dst, r_c + (flow * 4 + k - 1) * 2 + way)
                for i in range(32):
                    ih, iy, ic = i // 16, i // 2 % 8, i % 2
                    bx[pl.ds(i * 16, 16), :] = xbuf[iy % 4 * 2 + iy // 4, ih, ic, pl.ds(64, 16), :]
                lax.fori_loop(0, NL, rot_x, 0)
            elif name == "C0":
                columns(0).start()

        h0, h1 = pl.ds(0, 64), pl.ds(64, 64)
        pass_on(gbuf.at[g_own, h0], r_g, xp)
        pass_on(gbuf.at[g_own, h1], r_g + 1, xm)
        for q in range(2):
            own_z(b_part(zl, q), r_b + 2 * zl + q)
        pass_on(x_own, r_y, yp)
        pass_on(x_own, r_y + 1, ym)
        pass_on(x_own, r_co, co)
        pass_on(gbuf.at[g_own, h1], r_g + 2, xp)
        pass_on(gbuf.at[g_own, h0], r_g + 3, xm)
        for name in order:
            event(name)

    def both(finish):
        pl.when(inner == 0)(lambda: program(False, END_ORDER, finish))
        pl.when(inner == 1)(lambda: program(True, INNER_ORDER, finish))

    both(False)
    outs = []
    for i in range(NL):
        for h in range(2):
            if along_plus(i, h):
                arrived(rt.at[1, slots[i], BZ_ROWS if h else A_ROWS], r_x + 4 * i + 2 * h + 1)
    outs.append(columns(1))
    outs[-1].start()
    for i in range(NL):
        for h in range(2):
            if not along_plus(i, h):
                arrived(rt.at[3, slots[i], BZ_ROWS if h else A_ROWS], r_x + 4 * i + 2 * h)
    outs.append(columns(3))
    outs[-1].start()
    for i in range(NL):
        for h in range(2):
            arrived(rt.at[2, slots[i], BZ_ROWS if h else A_ROWS], r_f + 2 * i + h)
    outs.append(columns(2))
    outs[-1].start()

    both(True)
    col = pl.ds(pl.multiple_of(x * 256, 256), 256)
    outs.append(pltpu.make_async_copy(out.at[:, col], o_ref.at[:, col], out_sem.at[0]))
    for cp in outs:
        cp.wait()


def per_device(activations, out_grads, in_basis, out_basis):
    bf = jnp.bfloat16
    hbm = pl.BlockSpec(memory_space=pl.ANY)
    return pl.pallas_call(
        kernel,
        out_shape=jax.ShapeDtypeStruct((512, 1024), jnp.float32),
        in_specs=[hbm] * 4,
        out_specs=hbm,
        scratch_shapes=[
            pltpu.VMEM((512, 1024), jnp.float32),
            pltpu.VMEM((NY, NH, 2, XROWS, 512), bf),
            pltpu.VMEM((NX, 128, 1024), bf),
            pltpu.VMEM((NL, 64, 1024), bf),
            pltpu.VMEM((NX, NL, 256, 512), bf),
            pltpu.VMEM((512, 512), bf),
            pltpu.VMEM((NL, 512, 512), bf),
            pltpu.VMEM((NL, 512, 512), bf),
            pltpu.SemaphoreType.DMA((110,)),
            pltpu.SemaphoreType.DMA((100,)),
            pltpu.SemaphoreType.DMA((4,)),
            pltpu.SemaphoreType.DMA((4,)),
        ],
        compiler_params=pltpu.CompilerParams(
            collective_id=0, has_side_effects=True, vmem_limit_bytes=60 * 2**20),
        cost_estimate=pl.CostEstimate(
            flops=6 * 10**9, bytes_accessed=4 * 2**20, transcendentals=0),
        name="gather_and_scale",
    )(activations, in_basis.T, out_grads, out_basis.T)


def solution(mesh):
    in_specs = (P("fsdp", "rep"), P("rep", "fsdp"), P("rep", "fsdp"), P("fsdp", "rep"))
    out_specs = P("rep", "fsdp")
    return jax.shard_map(
        per_device, mesh=mesh, in_specs=in_specs, out_specs=out_specs, check_vma=False
    )
```

time: 328 us -> 63.6 us (0.19); the launches traced: 324 us -> 63.5 us
  waiting for transfers between devices: 249 us -> 0 us
  Pallas kernels: 0 us -> 60.3 us
  blocking collectives: 47.3 us -> 0 us
  matrix products: 14.4 us -> 0 us
  between operations: 13.1 us -> 0.01 us
    all_gather x3 -> x0, waiting for transfers between devices: 248 us -> none  [the longest x1 107 us: per_device(): piece = lax.all_gather(rot_g, 'rep', axis=0, tiled=True)]
    pallas_call x0 -> x1, Pallas kernels: none -> 60.3 us  [per_device(): pl.pallas_call(kernel, out_shape=jax.ShapeDtypeStruct((512, 1024), jnp.fl...]
    all_gather x1 -> x0, blocking collectives: 47.3 us -> none  [per_device(): in_cols = lax.all_gather(in_basis, 'fsdp', axis=1, tiled=True)]
    dot_general x4 -> x0, matrix products: 14.4 us -> none  [the longest x2 5.87 us: rotate(): jnp.einsum('tkb,kbc->tkc', parts, blocks, preferred_element_type=jnp.floa...]
  transfers between devices with their start and end apart: 3 -> 0, of which waited for: 3 -> 0; matrix products, arithmetic and copies ran while one was open for 2% -> 0% of each run, Pallas kernels for 0% -> 0%
where the time goes in v3:
time: 63.6 us; the launch traced here: 63.5 us
  Pallas kernels  60.3 us (95%)
  local copies, waits for them, and re-layouts  3.16 us (5%)
    pallas_call x1, Pallas kernels, per_device(): pl.pallas_call(kernel, out_shape=jax.ShapeDtypeStruct((512, 1024), jnp.fl...  60.3 us
    unnamed x1, local copies, waits for them, and re-layouts  3.16 us

profile of v3, /device:TPU:56, one launch (start us, length us, event | category | flops | bytes accessed | tf_op | source)
XLA Modules:
  0.0 63.5 jit_solution(17609345936739116731)
XLA Ops:
  0.0 60.3 %gather_and_scale.1 = f32[512,1024]{1,0:T(8,128)} custom-call(bf16[64,512]{1,0:T(8,128)(2,1)} %x_ref.1, bf16[16,512]{1,0:T(8,128)(2,1)} %bitcast.3, bf16[128,1024]{1,0:T(8,128)(2,1)} %g_ref.1, bf16[64,1024]{1,0:T(8,128)(2,1)} %bitcast.2), custom_call_target="tpu_custom_call" | custom-call | flops 6000000000 | bytes 4194304 | tf_op jit(solution)/shard_map/gather_and_scale/pallas_call | solution.py:328
  60.3 3.2 %copy.6 = f32[512,1024]{1,0:T(8,128)} copy(f32[512,1024]{1,0:T(8,128)} %gather_and_scale.1) | data formatting | bytes 4194304

commit v4 on v3

--- a/solution.py
+++ b/solution.py
@@ -20,14 +20,14 @@
 LEFT, RIGHT = pl.ds(0, 256), pl.ds(256, 256)
 NT = (((1,), (1,)), ((), ()))
 END_ORDER = (
-    "Z4", "B0", "G2", "Y01", "G1", "GA", "XZ", "B1", "B2", "GB", "Y02", "WX", "Y11", "T0A",
-    "WF", "T0B", "Y12", "Y03", "T1A", "F1A", "WZ", "F0B", "T1B", "Y04", "F0A", "Y13", "T2A",
-    "Y14", "T2B", "F1B", "RX", "V1", "F2B", "V0", "V2", "F2A", "C0", "F3B", "F3A",
+    "L1", "L2", "G1", "L3", "Z4", "Y01", "G2", "B0", "GA", "B1", "B2", "GB", "WX", "XZ", "Y02",
+    "T0A", "Y11", "WF", "T0B", "Y03", "T1A", "WZ", "Y12", "T1B", "Y04", "Y13", "F1A", "F2A",
+    "F0B", "Y14", "T2A", "T2B", "F2B", "F1B", "F0A", "RX", "C0", "F3B", "V1", "V2", "V0", "F3A",
 )
 INNER_ORDER = (
-    "B1", "B0", "G1", "G2", "Z4", "Y01", "B2", "GA", "GB", "Y02", "XZ", "WX", "T0A", "T1A",
-    "Y03", "WF", "Y11", "T1B", "T0B", "T2A", "F1A", "F0B", "Y12", "Y04", "T2B", "WZ", "V0",
-    "Y13", "F0A", "V1", "F1B", "F2B", "Y14", "F2A", "F3A", "V2", "RX", "F3B", "C0",
+    "L1", "L2", "B1", "B0", "L3", "Z4", "G2", "G1", "B2", "GA", "GB", "Y01", "XZ", "WX", "T1A",
+    "T0A", "Y02", "Y11", "WF", "T0B", "T1B", "Y03", "T2A", "F0A", "Y12", "T2B", "WZ", "Y13",
+    "F1B", "V0", "F0B", "F1A", "Y04", "F2B", "Y14", "V1", "F2A", "V2", "RX", "C0", "F3A", "F3B",
 )
 
 
@@ -48,7 +48,7 @@
     return (h + i) % 2 == 0
 
 
-def kernel(x_ref, i_ref, g_ref, bt_ref, o_ref, out, xbuf, gbuf, bbuf, rt, bx, rx, sx, send_sem, recv_sem, own_sem, out_sem):
+def kernel(own_ref, out, xbuf, gbuf, bbuf, rt, bx, rx, sx, acc, send_sem, recv_sem, own_sem, level):
     rep, f = lax.axis_index("rep"), lax.axis_index("fsdp")
     x, zl = rep // NL, rep % NL
     zh, y, c = f // 16, (f // 2) % NY, f % 2
@@ -59,6 +59,9 @@
     slots = (zl,) + arrivals
     nb1 = (x * NL + arrivals[0], f)
     nb2 = (x * NL + (3 - zl), f)
+    z = zh * NL + zl
+    zp, zm = (
+        (x * NL + (z + d) % 8 % NL, (z + d) % 8 // NL * 16 + y * 2 + c) for d in (1, 7))
     yp = (rep, zh * 16 + ((y + 1) % NY) * 2 + c)
     ym = (rep, zh * 16 + ((y + 7) % NY) * 2 + c)
     z4 = (rep, (1 - zh) * 16 + y * 2 + c)
@@ -87,26 +90,30 @@
     def arrived(dst, r):
         copy(dst, dst, 0, r, xp).wait_recv()
 
+    partners = (xp, xm, zp, zm, yp, ym, co)
     barrier = pltpu.get_barrier_semaphore()
-    for dev in (xp, xm, nb1, yp, ym, z4, co):
+    for dev in partners:
         pl.semaphore_signal(barrier, inc=1, device_id=dev, device_id_type=MESH)
-
-    @pl.when(inner == 1)
-    def _():
-        pl.semaphore_signal(barrier, inc=1, device_id=nb2, device_id_type=MESH)
 
     x_own = xbuf.at[ys[0], zh, c]
     load = [
-        pltpu.make_async_copy(g_ref, gbuf.at[g_own], own_sem.at[0]),
-        pltpu.make_async_copy(bt_ref, bbuf.at[zl], own_sem.at[1]),
-        pltpu.make_async_copy(x_ref, x_own.at[pl.ds(0, 64)], own_sem.at[2]),
-        pltpu.make_async_copy(i_ref, x_own.at[pl.ds(64, 16)], own_sem.at[3]),
+        pltpu.make_async_copy(own_ref.at[pl.ds(0, 128)], gbuf.at[g_own], own_sem.at[0]),
+        pltpu.make_async_copy(own_ref.at[pl.ds(128, 64)], bbuf.at[zl], own_sem.at[1]),
+        pltpu.make_async_copy(
+            own_ref.at[pl.ds(192, 48), pl.ds(0, 512)], x_own.at[pl.ds(0, 48)], own_sem.at[2]),
+        pltpu.make_async_copy(
+            own_ref.at[pl.ds(192, 32), pl.ds(512, 512)], x_own.at[pl.ds(48, 32)], own_sem.at[3]),
     ]
     for cp in load:
         cp.start()
     for cp in load:
         cp.wait()
-    pl.semaphore_wait(barrier, 7 + inner)
+    pl.semaphore_wait(barrier, len(partners))
+
+    def tell(k):
+        pl.semaphore_signal(level.at[k - 1], inc=1, device_id=zm, device_id_type=MESH)
+
+    tell(1)
 
     def rot_x(t, _):
         data = xbuf[pl.ds(t * 2, 2), :, :, pl.ds(0, 64), :].reshape(512, 512)
@@ -115,23 +122,34 @@
         sx[t] = square(turned)
         return 0
 
-    def columns(dx):
-        col = pl.ds(pl.multiple_of((x + dx) % NX * 256, 256), 256)
+    def columns(dx, blocks, begin=True, end=True):
+        cols = [
+            pl.ds(pl.multiple_of((x + dx) % NX * 256 + p * 128, 128), 128)
+            for p in (zl // 2, 1 - zl // 2)]
 
         def rows(m, _):
             here = pl.ds(pl.multiple_of(m * 256, 256), 256)
-            grad = jnp.zeros((256, 256), jnp.float32)
-            scale = jnp.zeros((256, 256), jnp.float32)
-            for t in range(NL):
+            if begin:
+                grad = jnp.zeros((256, 256), jnp.float32)
+                scale = jnp.zeros((256, 256), jnp.float32)
+            else:
+                grad, scale = acc[0, here, :], acc[1, here, :]
+            for i in blocks:
+                t = slots[i]
                 halves = [rt[dx, t, A_ROWS, :], rt[dx, t, B_ROWS, :]]
-                piece = jnp.concatenate(halves if t < 2 else halves[::-1], axis=0)
+                piece = jnp.concatenate(halves if i < 2 else halves[::-1], axis=0)
                 grad += dot_nt(rx[t, here, :], piece)
                 scale += dot_nt(sx[t, here, :], square(piece))
-            out[here, col] = (grad / TOKENS) / (scale / TOKENS + DAMPING)
+            if end:
+                result = (grad / TOKENS) / (scale / TOKENS + DAMPING)
+                out[here, cols[0]] = result[:, :128]
+                out[here, cols[1]] = result[:, 128:]
+            else:
+                acc[0, here, :] = grad
+                acc[1, here, :] = scale
             return 0
 
         lax.fori_loop(0, 2, rows, 0)
-        return pltpu.make_async_copy(out.at[:, col], o_ref.at[:, col], out_sem.at[dx])
 
     def program(inside, order, finish):
         count = [0]
@@ -196,7 +214,12 @@
 
         def event(name):
             kind = name[0]
-            if name == "Z4":
+            if kind == "L":
+                if not finish:
+                    pl.semaphore_wait(level.at[int(name[1]) - 1], 1)
+                    if name != "L3":
+                        tell(int(name[1]) + 1)
+            elif name == "Z4":
                 pass_on(x_own, r_zh, z4)
             elif name == "XZ":
                 far = xbuf.at[ys[0], 1 - zh, c]
@@ -276,7 +299,7 @@
                     bx[pl.ds(i * 16, 16), :] = xbuf[iy % 4 * 2 + iy // 4, ih, ic, pl.ds(64, 16), :]
                 lax.fori_loop(0, NL, rot_x, 0)
             elif name == "C0":
-                columns(0).start()
+                columns(0, range(NL))
 
         h0, h1 = pl.ds(0, 64), pl.ds(64, 64)
         pass_on(gbuf.at[g_own, h0], r_g, xp)
@@ -296,42 +319,36 @@
         pl.when(inner == 1)(lambda: program(True, INNER_ORDER, finish))
 
     both(False)
-    outs = []
     for i in range(NL):
         for h in range(2):
             if along_plus(i, h):
                 arrived(rt.at[1, slots[i], BZ_ROWS if h else A_ROWS], r_x + 4 * i + 2 * h + 1)
-    outs.append(columns(1))
-    outs[-1].start()
+    columns(1, range(NL))
     for i in range(NL):
         for h in range(2):
             if not along_plus(i, h):
                 arrived(rt.at[3, slots[i], BZ_ROWS if h else A_ROWS], r_x + 4 * i + 2 * h)
-    outs.append(columns(3))
-    outs[-1].start()
-    for i in range(NL):
-        for h in range(2):
-            arrived(rt.at[2, slots[i], BZ_ROWS if h else A_ROWS], r_f + 2 * i + h)
-    outs.append(columns(2))
-    outs[-1].start()
-
+    columns(3, range(NL))
+    for blocks in ((0, 1, 2), (3,)):
+        for i in blocks:
+            for h in range(2):
+                arrived(rt.at[2, slots[i], BZ_ROWS if h else A_ROWS], r_f + 2 * i + h)
+        columns(2, blocks, begin=0 in blocks, end=3 in blocks)
     both(True)
-    col = pl.ds(pl.multiple_of(x * 256, 256), 256)
-    outs.append(pltpu.make_async_copy(out.at[:, col], o_ref.at[:, col], out_sem.at[0]))
-    for cp in outs:
-        cp.wait()
 
 
 def per_device(activations, out_grads, in_basis, out_basis):
     bf = jnp.bfloat16
-    hbm = pl.BlockSpec(memory_space=pl.ANY)
+    vmem = pl.BlockSpec(memory_space=pltpu.VMEM)
+    right = jnp.concatenate([activations[48:], in_basis.T, jnp.zeros((16, 512), bf)], axis=0)
+    wide = jnp.concatenate([activations[:48], right], axis=1)
+    own = jnp.concatenate([out_grads, out_basis.T, wide], axis=0)
     return pl.pallas_call(
         kernel,
         out_shape=jax.ShapeDtypeStruct((512, 1024), jnp.float32),
-        in_specs=[hbm] * 4,
-        out_specs=hbm,
+        in_specs=[vmem],
+        out_specs=vmem,
         scratch_shapes=[
-            pltpu.VMEM((512, 1024), jnp.float32),
             pltpu.VMEM((NY, NH, 2, XROWS, 512), bf),
             pltpu.VMEM((NX, 128, 1024), bf),
             pltpu.VMEM((NL, 64, 1024), bf),
@@ -339,17 +356,18 @@
             pltpu.VMEM((512, 512), bf),
             pltpu.VMEM((NL, 512, 512), bf),
             pltpu.VMEM((NL, 512, 512), bf),
+            pltpu.VMEM((2, 512, 256), jnp.float32),
             pltpu.SemaphoreType.DMA((110,)),
             pltpu.SemaphoreType.DMA((100,)),
             pltpu.SemaphoreType.DMA((4,)),
-            pltpu.SemaphoreType.DMA((4,)),
+            pltpu.SemaphoreType.REGULAR((3,)),
         ],
         compiler_params=pltpu.CompilerParams(
-            collective_id=0, has_side_effects=True, vmem_limit_bytes=60 * 2**20),
+            collective_id=0, has_side_effects=True, vmem_limit_bytes=48 * 2**20),
         cost_estimate=pl.CostEstimate(
             flops=6 * 10**9, bytes_accessed=4 * 2**20, transcendentals=0),
         name="gather_and_scale",
-    )(activations, in_basis.T, out_grads, out_basis.T)
+    )(own)
 
 
 def solution(mesh):

time: 63.6 us -> 61.7 us (0.970); the launches traced: 63.5 us -> 60.9 us
  Pallas kernels: 60.3 us -> 57 us
  other arithmetic: 0 us -> 1.07 us
    pallas_call x1, Pallas kernels: 60.3 us -> 57 us  [per_device(): pl.pallas_call(kernel, out_shape=jax.ShapeDtypeStruct((512, 1024), jnp.fl...]
    unnamed x1, local copies, waits for them, and re-layouts: 3.16 us -> 1.32 us
    slice x0 -> x2, local copies, waits for them, and re-layouts: none -> 1.52 us  [the longest x1 0.8 us: per_device(): wide = jnp.concatenate([activations[:48], right], axis=1)]
    concatenate x0 -> x1, other arithmetic: none -> 1.07 us  [per_device(): own = jnp.concatenate([out_grads, out_basis.T, wide], axis=0)]
where the time goes in v4:
time: 61.7 us; the launch traced here: 60.9 us
  Pallas kernels  57 us (92%)
  local copies, waits for them, and re-layouts  2.85 us (5%)
  other arithmetic  1.07 us (2%)
    pallas_call x1, Pallas kernels, per_device(): pl.pallas_call(kernel, out_shape=jax.ShapeDtypeStruct((512, 1024), jnp.fl...  57 us
    unnamed x1, local copies, waits for them, and re-layouts  1.32 us

profile of v4, /device:TPU:56, one launch (start us, length us, event | category | flops | bytes accessed | tf_op | source)
XLA Modules:
  0.0 60.9 jit_solution(17975448737488450013)
XLA Ops:
  0.0 0.7 %slice.7 = bf16[16,512]{1,0:T(8,128)(2,1)S(1)} slice(bf16[64,512]{1,0:T(8,128)(2,1)} %param.4), slice={[48:64], [0:512]} | slice | bytes 32768 | tf_op jit(solution)/shard_map/slice | solution.py:343
  0.7 0.8 %slice.6 = bf16[48,512]{1,0:T(8,128)(2,1)S(1)} slice(bf16[64,512]{1,0:T(8,128)(2,1)} %param.4), slice={[0:48], [0:512]} | slice | bytes 98304 | tf_op jit(solution)/shard_map/slice | solution.py:344
  1.5 1.1 %maximum_maximum_fusion.own_ref = bf16[240,1024]{1,0:T(8,128)(2,1)S(1)} fusion(bf16[16,512]{1,0:T(8,128)(2,1)S(1)} %broadcast_in_dim.3, bf16[16,512]{1,0:T(8,128)(2,1)} %bitcast.3, bf16[16,512]{1,0:T(8,128)(2,1)S(1)} %slice.7, bf16[48,512]{1,0:T(8,128)(2,1)S(1)} %slice.6, bf16[64,1024]{1,0:T(8,128)(2,1)} %bitcast.2, bf16[128,1024]{1,0:T(8,128)(2,1)} %param.5), kind=kLoop, calls=%fused_computation | loop fusion | flops 2949120 | bytes 983040 | tf_op jit(solution)/shard_map/concatenate | solution.py:345
  2.6 57.0 %gather_and_scale.1 = f32[512,1024]{1,0:T(8,128)S(1)} custom-call(bf16[240,1024]{1,0:T(8,128)(2,1)S(1)} %maximum_maximum_fusion.own_ref), custom_call_target="tpu_custom_call" | custom-call | flops 6000000000 | bytes 4194304 | tf_op jit(solution)/shard_map/gather_and_scale/pallas_call | solution.py:346
  59.6 1.3 %copy.6 = f32[512,1024]{1,0:T(8,128)} copy(f32[512,1024]{1,0:T(8,128)S(1)} %gather_and_scale.1) | data formatting | bytes 4194304
  (1 shorter events, 0.0 us)

commit v5 on v4

--- a/solution.py
+++ b/solution.py
@@ -12,7 +12,7 @@
 TOKENS = 2048
 NX, NL, NH, NY = 4, 4, 2, 8
 XROWS = 80
-WROWS = 32
+WROWS = 48
 A_ROWS = pl.ds(0, 128)
 B_ROWS = pl.ds(128, 128)
 BZ_ROWS = pl.ds(128, 128 - WROWS)
@@ -20,14 +20,14 @@
 LEFT, RIGHT = pl.ds(0, 256), pl.ds(256, 256)
 NT = (((1,), (1,)), ((), ()))
 END_ORDER = (
-    "L1", "L2", "G1", "L3", "Z4", "Y01", "G2", "B0", "GA", "B1", "B2", "GB", "WX", "XZ", "Y02",
-    "T0A", "Y11", "WF", "T0B", "Y03", "T1A", "WZ", "Y12", "T1B", "Y04", "Y13", "F1A", "F2A",
-    "F0B", "Y14", "T2A", "T2B", "F2B", "F1B", "F0A", "RX", "C0", "F3B", "V1", "V2", "V0", "F3A",
+    "L1", "L2", "Y01", "G1", "G2", "L3", "Z4", "B0", "B1", "Y02", "GA", "Y03", "B2", "GB", "XZ",
+    "WX", "T0A", "Y11", "WF", "T0B", "T1A", "WZ", "Y12", "T1B", "F0A", "F0B", "T2A", "F1B",
+    "Y13", "F1A", "Y04", "Y14", "T2B", "F2A", "F3A", "RX", "F2B", "V1", "V0", "F3B", "C0", "V2",
 )
 INNER_ORDER = (
-    "L1", "L2", "B1", "B0", "L3", "Z4", "G2", "G1", "B2", "GA", "GB", "Y01", "XZ", "WX", "T1A",
-    "T0A", "Y02", "Y11", "WF", "T0B", "T1B", "Y03", "T2A", "F0A", "Y12", "T2B", "WZ", "Y13",
-    "F1B", "V0", "F0B", "F1A", "Y04", "F2B", "Y14", "V1", "F2A", "V2", "RX", "C0", "F3A", "F3B",
+    "L1", "L2", "B1", "B0", "G2", "L3", "G1", "Z4", "Y01", "B2", "GA", "Y02", "GB", "XZ", "WX",
+    "Y03", "T0A", "T1A", "Y11", "WF", "T1B", "T0B", "F0A", "T2A", "Y12", "WZ", "Y13", "Y04",
+    "T2B", "F2A", "F2B", "V0", "Y14", "F0B", "F1A", "F1B", "V1", "F3A", "V2", "RX", "F3B", "C0",
 )
 
 
@@ -99,10 +99,7 @@
     load = [
         pltpu.make_async_copy(own_ref.at[pl.ds(0, 128)], gbuf.at[g_own], own_sem.at[0]),
         pltpu.make_async_copy(own_ref.at[pl.ds(128, 64)], bbuf.at[zl], own_sem.at[1]),
-        pltpu.make_async_copy(
-            own_ref.at[pl.ds(192, 48), pl.ds(0, 512)], x_own.at[pl.ds(0, 48)], own_sem.at[2]),
-        pltpu.make_async_copy(
-            own_ref.at[pl.ds(192, 32), pl.ds(512, 512)], x_own.at[pl.ds(48, 32)], own_sem.at[3]),
+        pltpu.make_async_copy(own_ref.at[pl.ds(192, XROWS), pl.ds(0, 512)], x_own, own_sem.at[2]),
     ]
     for cp in load:
         cp.start()
@@ -340,9 +337,9 @@
 def per_device(activations, out_grads, in_basis, out_basis):
     bf = jnp.bfloat16
     vmem = pl.BlockSpec(memory_space=pltpu.VMEM)
-    right = jnp.concatenate([activations[48:], in_basis.T, jnp.zeros((16, 512), bf)], axis=0)
-    wide = jnp.concatenate([activations[:48], right], axis=1)
-    own = jnp.concatenate([out_grads, out_basis.T, wide], axis=0)
+    pads = ((0, 0), (0, 512))
+    own = jnp.concatenate(
+        [out_grads, out_basis.T, jnp.pad(activations, pads), jnp.pad(in_basis.T, pads)], axis=0)
     return pl.pallas_call(
         kernel,
         out_shape=jax.ShapeDtypeStruct((512, 1024), jnp.float32),
@@ -359,7 +356,7 @@
             pltpu.VMEM((2, 512, 256), jnp.float32),
             pltpu.SemaphoreType.DMA((110,)),
             pltpu.SemaphoreType.DMA((100,)),
-            pltpu.SemaphoreType.DMA((4,)),
+            pltpu.SemaphoreType.DMA((3,)),
             pltpu.SemaphoreType.REGULAR((3,)),
         ],
         compiler_params=pltpu.CompilerParams(

time: 61.7 us -> 61.7 us (level)
  local copies, waits for them, and re-layouts: 2.85 us -> 1.32 us
  Pallas kernels: 57 us -> 58.1 us
    slice x2 -> x0, local copies, waits for them, and re-layouts: 1.52 us -> none  [the longest x1 0.8 us: per_device(): wide = jnp.concatenate([activations[:48], right], axis=1)]
    pallas_call x1, Pallas kernels: 57 us -> 58.1 us  [per_device(): pl.pallas_call(kernel, out_shape=jax.ShapeDtypeStruct((512, 1024), jnp.fl...]
where the time goes in v5:
time: 61.7 us; the launch traced here: 60.5 us
  Pallas kernels  58.1 us (94%)
  local copies, waits for them, and re-layouts  1.32 us (2%)
  other arithmetic  1.12 us (2%)
    pallas_call x1, Pallas kernels, per_device(): pl.pallas_call(kernel, out_shape=jax.ShapeDtypeStruct((512, 1024), jnp.fl...  58.1 us
    unnamed x1, local copies, waits for them, and re-layouts  1.32 us

profile of v5, /device:TPU:56, one launch (start us, length us, event | category | flops | bytes accessed | tf_op | source)
XLA Modules:
  0.0 60.5 jit_solution(476801433628462748)
XLA Ops:
  0.0 1.1 %fusion.4.own_ref = bf16[272,1024]{1,0:T(8,128)(2,1)S(1)} fusion(bf16[16,512]{1,0:T(8,128)(2,1)} %bitcast.3, bf16[64,512]{1,0:T(8,128)(2,1)} %param.4, bf16[64,1024]{1,0:T(8,128)(2,1)} %bitcast.2, bf16[128,1024]{1,0:T(8,128)(2,1)} %param.5), kind=kLoop, calls=%fused_computation.7 | loop fusion | flops 3899392 | bytes 1032192 | tf_op jit(solution)/shard_map/concatenate | solution.py:341
  1.1 58.1 %gather_and_scale.1 = f32[512,1024]{1,0:T(8,128)S(1)} custom-call(bf16[272,1024]{1,0:T(8,128)(2,1)S(1)} %fusion.4.own_ref), custom_call_target="tpu_custom_call" | custom-call | flops 6000000000 | bytes 4194304 | tf_op jit(solution)/shard_map/gather_and_scale/pallas_call | solution.py:343
  59.2 1.3 %copy.6 = f32[512,1024]{1,0:T(8,128)} copy(f32[512,1024]{1,0:T(8,128)S(1)} %gather_and_scale.1) | data formatting | bytes 4194304

commit v6 on v5

--- a/solution.py
+++ b/solution.py
@@ -22,12 +22,12 @@
 END_ORDER = (
     "L1", "L2", "Y01", "G1", "G2", "L3", "Z4", "B0", "B1", "Y02", "GA", "Y03", "B2", "GB", "XZ",
     "WX", "T0A", "Y11", "WF", "T0B", "T1A", "WZ", "Y12", "T1B", "F0A", "F0B", "T2A", "F1B",
-    "Y13", "F1A", "Y04", "Y14", "T2B", "F2A", "F3A", "RX", "F2B", "V1", "V0", "F3B", "C0", "V2",
+    "Y13", "F1A", "Y04", "Y14", "T2B", "F2A", "F3A", "RX", "F2B", "V1", "V0", "F3B",  "V2",
 )
 INNER_ORDER = (
     "L1", "L2", "B1", "B0", "G2", "L3", "G1", "Z4", "Y01", "B2", "GA", "Y02", "GB", "XZ", "WX",
     "Y03", "T0A", "T1A", "Y11", "WF", "T1B", "T0B", "F0A", "T2A", "Y12", "WZ", "Y13", "Y04",
-    "T2B", "F2A", "F2B", "V0", "Y14", "F0B", "F1A", "F1B", "V1", "F3A", "V2", "RX", "F3B", "C0",
+    "T2B", "F2A", "F2B", "V0", "Y14", "F0B", "F1A", "F1B", "V1", "F3A", "V2", "RX", "F3B",
 )
 
 
@@ -295,8 +295,6 @@
                     ih, iy, ic = i // 16, i // 2 % 8, i % 2
                     bx[pl.ds(i * 16, 16), :] = xbuf[iy % 4 * 2 + iy // 4, ih, ic, pl.ds(64, 16), :]
                 lax.fori_loop(0, NL, rot_x, 0)
-            elif name == "C0":
-                columns(0, range(NL))
 
         h0, h1 = pl.ds(0, 64), pl.ds(64, 64)
         pass_on(gbuf.at[g_own, h0], r_g, xp)
@@ -316,6 +314,7 @@
         pl.when(inner == 1)(lambda: program(True, INNER_ORDER, finish))
 
     both(False)
+    columns(0, range(NL))
     for i in range(NL):
         for h in range(2):
             if along_plus(i, h):
@@ -327,11 +326,12 @@
                 arrived(rt.at[3, slots[i], BZ_ROWS if h else A_ROWS], r_x + 4 * i + 2 * h)
     columns(3, range(NL))
     for blocks in ((0, 1, 2), (3,)):
+        if 3 in blocks:
+            both(True)
         for i in blocks:
             for h in range(2):
                 arrived(rt.at[2, slots[i], BZ_ROWS if h else A_ROWS], r_f + 2 * i + h)
         columns(2, blocks, begin=0 in blocks, end=3 in blocks)
-    both(True)
 
 
 def per_device(activations, out_grads, in_basis, out_basis):

time: 61.7 us -> 61.7 us (level)
  no operation moved by 1% of the time
where the time goes in v6:
time: 61.7 us; the launch traced here: 60.5 us
  Pallas kernels  58.1 us (94%)
  local copies, waits for them, and re-layouts  1.32 us (2%)
  other arithmetic  1.12 us (2%)
    pallas_call x1, Pallas kernels, per_device(): pl.pallas_call(kernel, out_shape=jax.ShapeDtypeStruct((512, 1024), jnp.fl...  58.1 us
    unnamed x1, local copies, waits for them, and re-layouts  1.32 us

profile of v6, /device:TPU:56, one launch (start us, length us, event | category | flops | bytes accessed | tf_op | source)
XLA Modules:
  0.0 60.5 jit_solution(3608707319063149553)
XLA Ops:
  0.0 1.1 %fusion.4.own_ref = bf16[272,1024]{1,0:T(8,128)(2,1)S(1)} fusion(bf16[16,512]{1,0:T(8,128)(2,1)} %bitcast.3, bf16[64,512]{1,0:T(8,128)(2,1)} %param.4, bf16[64,1024]{1,0:T(8,128)(2,1)} %bitcast.2, bf16[128,1024]{1,0:T(8,128)(2,1)} %param.5), kind=kLoop, calls=%fused_computation.7 | loop fusion | flops 3899392 | bytes 1032192 | tf_op jit(solution)/shard_map/concatenate | solution.py:341
  1.1 58.1 %gather_and_scale.1 = f32[512,1024]{1,0:T(8,128)S(1)} custom-call(bf16[272,1024]{1,0:T(8,128)(2,1)S(1)} %fusion.4.own_ref), custom_call_target="tpu_custom_call" | custom-call | flops 6000000000 | bytes 4194304 | tf_op jit(solution)/shard_map/gather_and_scale/pallas_call | solution.py:343
  59.2 1.3 %copy.6 = f32[512,1024]{1,0:T(8,128)} copy(f32[512,1024]{1,0:T(8,128)S(1)} %gather_and_scale.1) | data formatting | bytes 4194304

commit v7 on v6

--- a/solution.py
+++ b/solution.py
@@ -20,14 +20,14 @@
 LEFT, RIGHT = pl.ds(0, 256), pl.ds(256, 256)
 NT = (((1,), (1,)), ((), ()))
 END_ORDER = (
-    "L1", "L2", "Y01", "G1", "G2", "L3", "Z4", "B0", "B1", "Y02", "GA", "Y03", "B2", "GB", "XZ",
-    "WX", "T0A", "Y11", "WF", "T0B", "T1A", "WZ", "Y12", "T1B", "F0A", "F0B", "T2A", "F1B",
-    "Y13", "F1A", "Y04", "Y14", "T2B", "F2A", "F3A", "RX", "F2B", "V1", "V0", "F3B",  "V2",
+    "G1", "Y01", "B0", "Z4", "G2", "Y02", "GA", "B1", "B2", "GB", "XZ", "Y03", "WX", "T0A",
+    "Y11", "WF", "T0B", "F0A", "T1A", "Y04", "F0B", "WZ", "Y12", "T1B", "Y13", "T2A", "T2B",
+    "F2A", "Y14", "F2B", "F1A", "V0", "F1B", "F3A", "RX", "F3B", "V1", "V2",
 )
 INNER_ORDER = (
-    "L1", "L2", "B1", "B0", "G2", "L3", "G1", "Z4", "Y01", "B2", "GA", "Y02", "GB", "XZ", "WX",
-    "Y03", "T0A", "T1A", "Y11", "WF", "T1B", "T0B", "F0A", "T2A", "Y12", "WZ", "Y13", "Y04",
-    "T2B", "F2A", "F2B", "V0", "Y14", "F0B", "F1A", "F1B", "V1", "F3A", "V2", "RX", "F3B",
+    "Z4", "G1", "B0", "G2", "Y01", "B1", "B2", "GA", "Y02", "GB", "WX", "XZ", "T0A", "T1A",
+    "Y03", "Y11", "WF", "T1B", "T0B", "Y04", "Y12", "T2A", "T2B", "WZ", "Y13", "F2A", "V0",
+    "F1B", "Y14", "F0B", "F2B", "F0A", "F1A", "V1", "F3B", "V2", "RX", "F3A",
 )
 
 
@@ -48,7 +48,7 @@
     return (h + i) % 2 == 0
 
 
-def kernel(own_ref, out, xbuf, gbuf, bbuf, rt, bx, rx, sx, acc, send_sem, recv_sem, own_sem, level):
+def kernel(own_ref, out, xbuf, gbuf, bbuf, rt, bx, rx, sx, acc, send_sem, recv_sem, own_sem):
     rep, f = lax.axis_index("rep"), lax.axis_index("fsdp")
     x, zl = rep // NL, rep % NL
     zh, y, c = f // 16, (f // 2) % NY, f % 2
@@ -90,7 +90,7 @@
     def arrived(dst, r):
         copy(dst, dst, 0, r, xp).wait_recv()
 
-    partners = (xp, xm, zp, zm, yp, ym, co)
+    partners = (xp, xm, zp, zm, z4, yp, ym, co)
     barrier = pltpu.get_barrier_semaphore()
     for dev in partners:
         pl.semaphore_signal(barrier, inc=1, device_id=dev, device_id_type=MESH)
@@ -106,11 +106,6 @@
     for cp in load:
         cp.wait()
     pl.semaphore_wait(barrier, len(partners))
-
-    def tell(k):
-        pl.semaphore_signal(level.at[k - 1], inc=1, device_id=zm, device_id_type=MESH)
-
-    tell(1)
 
     def rot_x(t, _):
         data = xbuf[pl.ds(t * 2, 2), :, :, pl.ds(0, 64), :].reshape(512, 512)
@@ -211,12 +206,7 @@
 
         def event(name):
             kind = name[0]
-            if kind == "L":
-                if not finish:
-                    pl.semaphore_wait(level.at[int(name[1]) - 1], 1)
-                    if name != "L3":
-                        tell(int(name[1]) + 1)
-            elif name == "Z4":
+            if name == "Z4":
                 pass_on(x_own, r_zh, z4)
             elif name == "XZ":
                 far = xbuf.at[ys[0], 1 - zh, c]
@@ -357,7 +347,6 @@
             pltpu.SemaphoreType.DMA((110,)),
             pltpu.SemaphoreType.DMA((100,)),
             pltpu.SemaphoreType.DMA((3,)),
-            pltpu.SemaphoreType.REGULAR((3,)),
         ],
         compiler_params=pltpu.CompilerParams(
             collective_id=0, has_side_effects=True, vmem_limit_bytes=48 * 2**20),

time: 61.7 us -> 63.1 us (1.023); the launches traced: 60.5 us -> 62.8 us
  Pallas kernels: 58.1 us -> 60.4 us
    pallas_call x1, Pallas kernels: 58.1 us -> 60.4 us  [per_device(): pl.pallas_call(kernel, out_shape=jax.ShapeDtypeStruct((512, 1024), jnp.fl...]
where the time goes in v7:
time: 63.1 us; the launch traced here: 62.8 us
  Pallas kernels  60.4 us (96%)
  local copies, waits for them, and re-layouts  1.32 us (2%)
  other arithmetic  1.12 us (2%)
    pallas_call x1, Pallas kernels, per_device(): pl.pallas_call(kernel, out_shape=jax.ShapeDtypeStruct((512, 1024), jnp.fl...  60.4 us
    unnamed x1, local copies, waits for them, and re-layouts  1.32 us

profile of v7, /device:TPU:56, one launch (start us, length us, event | category | flops | bytes accessed | tf_op | source)
XLA Modules:
  0.0 62.8 jit_solution(15703920173892111585)
XLA Ops:
  0.0 1.1 %fusion.4.own_ref = bf16[272,1024]{1,0:T(8,128)(2,1)S(1)} fusion(bf16[16,512]{1,0:T(8,128)(2,1)} %bitcast.3, bf16[64,512]{1,0:T(8,128)(2,1)} %param.4, bf16[64,1024]{1,0:T(8,128)(2,1)} %bitcast.2, bf16[128,1024]{1,0:T(8,128)(2,1)} %param.5), kind=kLoop, calls=%fused_computation.7 | loop fusion | flops 3899392 | bytes 1032192 | tf_op jit(solution)/shard_map/concatenate | solution.py:331
  1.1 60.4 %gather_and_scale.1 = f32[512,1024]{1,0:T(8,128)S(1)} custom-call(bf16[272,1024]{1,0:T(8,128)(2,1)S(1)} %fusion.4.own_ref), custom_call_target="tpu_custom_call" | custom-call | flops 6000000000 | bytes 4194304 | tf_op jit(solution)/shard_map/gather_and_scale/pallas_call | solution.py:333
  61.5 1.3 %copy.6 = f32[512,1024]{1,0:T(8,128)} copy(f32[512,1024]{1,0:T(8,128)S(1)} %gather_and_scale.1) | data formatting | bytes 4194304

commit v8 on v5

--- a/solution.py
+++ b/solution.py
@@ -48,7 +48,7 @@
     return (h + i) % 2 == 0
 
 
-def kernel(own_ref, out, xbuf, gbuf, bbuf, rt, bx, rx, sx, acc, send_sem, recv_sem, own_sem, level):
+def kernel(own_ref, out, xbuf, gbuf, bbuf, rt, bx, rx, sx, acc, sq, send_sem, recv_sem, own_sem, level):
     rep, f = lax.axis_index("rep"), lax.axis_index("fsdp")
     x, zl = rep // NL, rep % NL
     zh, y, c = f // 16, (f // 2) % NY, f % 2
@@ -124,6 +124,13 @@
             pl.ds(pl.multiple_of((x + dx) % NX * 256 + p * 128, 128), 128)
             for p in (zl // 2, 1 - zl // 2)]
 
+        def block(i):
+            halves = [rt[dx, slots[i], A_ROWS, :], rt[dx, slots[i], B_ROWS, :]]
+            return jnp.concatenate(halves if i < 2 else halves[::-1], axis=0)
+
+        for i in blocks:
+            sq[i] = square(block(i))
+
         def rows(m, _):
             here = pl.ds(pl.multiple_of(m * 256, 256), 256)
             if begin:
@@ -133,10 +140,8 @@
                 grad, scale = acc[0, here, :], acc[1, here, :]
             for i in blocks:
                 t = slots[i]
-                halves = [rt[dx, t, A_ROWS, :], rt[dx, t, B_ROWS, :]]
-                piece = jnp.concatenate(halves if i < 2 else halves[::-1], axis=0)
-                grad += dot_nt(rx[t, here, :], piece)
-                scale += dot_nt(sx[t, here, :], square(piece))
+                grad += dot_nt(rx[t, here, :], block(i))
+                scale += dot_nt(sx[t, here, :], sq[i])
             if end:
                 result = (grad / TOKENS) / (scale / TOKENS + DAMPING)
                 out[here, cols[0]] = result[:, :128]
@@ -354,6 +359,7 @@
             pltpu.VMEM((NL, 512, 512), bf),
             pltpu.VMEM((NL, 512, 512), bf),
             pltpu.VMEM((2, 512, 256), jnp.float32),
+            pltpu.VMEM((NL, 256, 512), bf),
             pltpu.SemaphoreType.DMA((110,)),
             pltpu.SemaphoreType.DMA((100,)),
             pltpu.SemaphoreType.DMA((3,)),

time: 61.7 us -> 62.3 us (level)
  no operation moved by 1% of the time
where the time goes in v8:
time: 62.3 us; the launch traced here: 61.1 us
  Pallas kernels  58.6 us (94%)
  local copies, waits for them, and re-layouts  1.32 us (2%)
  other arithmetic  1.12 us (2%)
    pallas_call x1, Pallas kernels, per_device(): pl.pallas_call(kernel, out_shape=jax.ShapeDtypeStruct((512, 1024), jnp.fl...  58.6 us
    unnamed x1, local copies, waits for them, and re-layouts  1.32 us

profile of v8, /device:TPU:56, one launch (start us, length us, event | category | flops | bytes accessed | tf_op | source)
XLA Modules:
  0.0 61.1 jit_solution(13127718718820334580)
XLA Ops:
  0.0 1.1 %fusion.4.own_ref = bf16[272,1024]{1,0:T(8,128)(2,1)S(1)} fusion(bf16[16,512]{1,0:T(8,128)(2,1)} %bitcast.3, bf16[64,512]{1,0:T(8,128)(2,1)} %param.4, bf16[64,1024]{1,0:T(8,128)(2,1)} %bitcast.2, bf16[128,1024]{1,0:T(8,128)(2,1)} %param.5), kind=kLoop, calls=%fused_computation.7 | loop fusion | flops 3899392 | bytes 1032192 | tf_op jit(solution)/shard_map/concatenate | solution.py:346
  1.1 58.6 %gather_and_scale.1 = f32[512,1024]{1,0:T(8,128)S(1)} custom-call(bf16[272,1024]{1,0:T(8,128)(2,1)S(1)} %fusion.4.own_ref), custom_call_target="tpu_custom_call" | custom-call | flops 6000000000 | bytes 4194304 | tf_op jit(solution)/shard_map/gather_and_scale/pallas_call | solution.py:348
  59.8 1.3 %copy.6 = f32[512,1024]{1,0:T(8,128)} copy(f32[512,1024]{1,0:T(8,128)S(1)} %gather_and_scale.1) | data formatting | bytes 4194304
